TPU v7x, 32 devices: a whole 2x2x4 slice. The times are simulated.
32 devices in a mesh: grp: 4 (over y, x), tm: 8 (over z, core).
Axes of the slice: x: 2, y: 2, z: 4, core: 2. Of those that a mesh axis runs over, the one named last changes fastest.
Arguments:
- signal: bfloat16 [4, 1024, 512], P('grp', 'tm'), may hold values from -6 to 6
- damping: float32 [4, 1024], P('grp', 'tm'), may hold values from 0.25 to 1, as said below
- nu_log: float32 [1024], replicated, as said below
- theta: float32 [1024], replicated, may hold values from 0 to 0.63
- in_weight: bfloat16 [512, 2048], replicated, may hold values from -0.25 to 0.25
- out_weight: bfloat16 [512, 2048], replicated, may hold values from -0.125 to 0.125
- skip_gain: float32 [512], replicated, may hold values from 0.1 to 1.9
- cotangent: bfloat16 [4, 1024, 512], P('grp', 'tm'), may hold values from -6 to 6
Outputs:
- mixed: bfloat16 [4, 1024, 512], P('grp', 'tm')
- grad_signal: bfloat16 [4, 1024, 512], P('grp', 'tm')
- grad_in: float32 [512, 2048], P(('grp', 'tm'))
- grad_out: float32 [512, 2048], P(('grp', 'tm'))
Inputs may be any that keep to these rules, and one draw needn't show every extreme that they name: damping is 1 except at a few time steps of each record. exp(nu_log) lies between 0.01 / 1024 and 1/30.
All inputs are finite; a program needn't handle non-finite values.
Results may differ from a plain program's by a relative error of at most 0.0034.
Values sent between devices are 32-bit elements; how exact they have to be, the bound alone decides.
A program may use at most 128 MiB of HBM per device.

v0:
```python
import math

import jax
import jax.numpy as jnp
from jax import lax
from jax.sharding import PartitionSpec as P


def prefix(part, axis, combine, identity, reverse):
    count = lax.axis_size(axis)
    place = lax.axis_index(axis)
    ahead = count - 1 - place if reverse else place
    gathered = jax.tree.map(lambda a: lax.all_gather(a, axis), part)
    state = jax.tree.map(lambda a, e: jnp.zeros_like(a) + jnp.asarray(e, a.dtype), part, identity)

    def one(turn, state):
        source = count - 1 - turn if reverse else turn
        return combine(
            state, jax.tree.map(lambda a: lax.dynamic_index_in_dim(a, source, 0, False), gathered)
        )

    return lax.fori_loop(0, ahead, one, state)


def combine(earlier, later):
    first_re, first_im, carry_re, carry_im = earlier
    second_re, second_im, next_re, next_im = later
    prod_re = second_re * first_re - second_im * first_im
    prod_im = second_re * first_im + second_im * first_re
    moved_re = second_re * carry_re - second_im * carry_im
    moved_im = second_re * carry_im + second_im * carry_re
    return (prod_re, prod_im, moved_re + next_re, moved_im + next_im)


def chain(decay_re, decay_im, drive_re, drive_im, backward):
    length, width = decay_re.shape
    inner = math.gcd(length, 16)
    outer = length // inner
    pieces = [
        item.reshape(outer, inner, width) for item in (decay_re, decay_im, drive_re, drive_im)
    ]
    carry = (
        jnp.ones((outer, width), jnp.float32),
        jnp.zeros((outer, width), jnp.float32),
        jnp.zeros((outer, width), jnp.float32),
        jnp.zeros((outer, width), jnp.float32),
    )
    order = list(range(inner))
    if backward:
        order = order[::-1]
    kept = {}
    for place in order:
        element = tuple((item[:, place] for item in pieces))
        carry = combine(carry, element)
        kept[place] = carry
    local = [jnp.stack([kept[place][member] for place in range(inner)], 1) for member in range(4)]
    summary = carry
    if backward:
        summary = tuple((jnp.flip(item, 0) for item in summary))
    inclusive = lax.associative_scan(combine, summary)
    ident = (
        jnp.ones((1, width), jnp.float32),
        jnp.zeros((1, width), jnp.float32),
        jnp.zeros((1, width), jnp.float32),
        jnp.zeros((1, width), jnp.float32),
    )
    exclusive = tuple(
        (
            jnp.concatenate([leading_operand, item[:-1]], 0)
            for leading_operand, item in zip(ident, inclusive)
        )
    )
    if backward:
        exclusive = tuple((jnp.flip(item, 0) for item in exclusive))
    enter_pre, enter_pim, enter_sre, enter_sim = [item[:, None, :] for item in exclusive]
    power_re, power_im, state_re, state_im = local
    total_re = state_re + power_re * enter_sre - power_im * enter_sim
    total_im = state_im + power_re * enter_sim + power_im * enter_sre
    whole_re = power_re * enter_pre - power_im * enter_pim
    whole_im = power_re * enter_pim + power_im * enter_pre
    return tuple((item.reshape(length, width) for item in (total_re, total_im, whole_re, whole_im)))


def body(signal, damping, nu_log, theta, in_weight, out_weight, skip_gain, cotangent):
    width = nu_log.shape[0]
    rate = jnp.exp(nu_log)
    magnitude = jnp.exp(-rate)
    lam_re = magnitude * jnp.cos(theta)
    lam_im = magnitude * jnp.sin(theta)
    scaling = jnp.sqrt(-jnp.expm1(-2.0 * rate))
    sig_rows = signal[0]
    upstream = cotangent[0]
    damp = damping[0][:, None]
    decay_re = damp * lam_re
    decay_im = damp * lam_im
    projected = jnp.dot(sig_rows, in_weight, preferred_element_type=jnp.float32)
    local_re, local_im, power_re, power_im = chain(
        decay_re, decay_im, scaling * projected[:, :width], scaling * projected[:, width:], False
    )
    grad_packed = jnp.dot(upstream, out_weight, preferred_element_type=jnp.float32)
    shift_re = jnp.concatenate([decay_re[1:], jnp.ones((1, width), jnp.float32)], 0)
    shift_im = jnp.concatenate([-decay_im[1:], jnp.zeros((1, width), jnp.float32)], 0)
    back_re, back_im, bpow_re, bpow_im = chain(
        shift_re, shift_im, grad_packed[:, :width], grad_packed[:, width:], True
    )
    forward_sum = (power_re[-1], power_im[-1], local_re[-1], local_im[-1])
    start_re = decay_re[0] * back_re[0] + decay_im[0] * back_im[0]
    start_im = decay_re[0] * back_im[0] - decay_im[0] * back_re[0]
    backward_sum = (power_re[-1], -power_im[-1], start_re, start_im)
    ident = (
        jnp.ones((width,), jnp.float32),
        jnp.zeros((width,), jnp.float32),
        jnp.zeros((width,), jnp.float32),
        jnp.zeros((width,), jnp.float32),
    )
    carry_fwd = prefix(forward_sum, "tm", combine, ident, False)
    carry_bwd = prefix(backward_sum, "tm", combine, ident, True)
    state_re = local_re + power_re * carry_fwd[2] - power_im * carry_fwd[3]
    state_im = local_im + power_re * carry_fwd[3] + power_im * carry_fwd[2]
    packed = jnp.concatenate([state_re, state_im], 1).astype(jnp.bfloat16)
    output = lax.dot_general(
        packed, out_weight, (((1,), (1,)), ((), ())), preferred_element_type=jnp.float32
    )
    output = (output + skip_gain * sig_rows.astype(jnp.float32)).astype(jnp.bfloat16)
    adj_re = back_re + bpow_re * carry_bwd[2] - bpow_im * carry_bwd[3]
    adj_im = back_im + bpow_re * carry_bwd[3] + bpow_im * carry_bwd[2]
    grad_drive = jnp.concatenate([scaling * adj_re, scaling * adj_im], 1).astype(jnp.bfloat16)
    grad_rows = lax.dot_general(
        grad_drive, in_weight, (((1,), (1,)), ((), ())), preferred_element_type=jnp.float32
    )
    grad_rows = (grad_rows + skip_gain * upstream.astype(jnp.float32)).astype(jnp.bfloat16)
    term_in = lax.dot_general(
        sig_rows, grad_drive, (((0,), (0,)), ((), ())), preferred_element_type=jnp.float32
    )
    term_out = lax.dot_general(
        upstream, packed, (((0,), (0,)), ((), ())), preferred_element_type=jnp.float32
    )
    summed = lax.psum_scatter(
        jnp.concatenate([term_in, term_out], 1), ("grp", "tm"), scatter_dimension=0, tiled=True
    )
    grad_in = summed[:, : 2 * width]
    grad_out = summed[:, 2 * width :]
    return (output[None], grad_rows[None], grad_in, grad_out)


def solution(mesh):
    placed = (P("grp", "tm", None), P("grp", "tm"), P(), P(), P(), P(), P(), P("grp", "tm", None))
    return jax.shard_map(
        body,
        mesh=mesh,
        in_specs=placed,
        out_specs=(
            P("grp", "tm", None),
            P("grp", "tm", None),
            P(("grp", "tm"), None),
            P(("grp", "tm"), None),
        ),
        check_vma=False,
    )
```

profile of v0, /device:TPU:0, one launch (start us, length us, event | category | flops | bytes accessed | tf_op | source)
XLA Modules:
  0.0 538.8 jit_solution(11617588272464098306)
XLA Ops:
  10.0 2.1 fusion.16
  63.4 3.8 slice.1022
  67.2 3.9 slice.1035
  71.2 3.9 slice.1019
  75.1 3.9 slice.1029
  79.0 4.0 slice.1017
  82.9 3.9 slice.1024
  86.9 4.0 slice.1027
  90.8 3.9 slice.1015
  113.2 2.5 constant_dynamic-update-slice_fusion.79
  143.8 3.9 slice.1062
  147.6 2.8 slice.1053
  150.4 3.8 slice.1058
  154.2 2.8 slice.1013
  162.6 2.4 rev.19
  166.5 2.4 rev.20
  175.9 2.4 rev.17
  179.9 2.4 rev.18
  235.2 15.7 %all-gather.6 = f32[8,1,1024]{2,1,0:T(1,128)S(1)} all-gather(f32[1,1,1024]{2,1,0:T(1,128)S(1)} %get-tuple-element.502), channel_id=1, replica_groups=mesh['grp'=4,'tm'=8] {'tm'}, dimensions={0}, use_global_device_ids=true | all-gather | bytes 36864 | tf_op jit(solution)/shard_map/all_gather | solution.py:13
  250.8 14.0 %all-gather.5 = f32[8,1,1024]{2,1,0:T(1,128)S(1)} all-gather(f32[1,1,1024]{2,1,0:T(1,128)S(1)} %get-tuple-element.503), channel_id=1, replica_groups=mesh['grp'=4,'tm'=8] {'tm'}, dimensions={0}, use_global_device_ids=true | all-gather | bytes 36864 | tf_op jit(solution)/shard_map/all_gather | solution.py:13
  282.7 1.8 multiply_add_fusion.2
  284.9 14.0 %all-gather.3 = f32[8,1,1024]{2,1,0:T(1,128)S(1)} all-gather(f32[1,1,1024]{2,1,0:T(1,128)S(1)} %slice_bitcast_fusion), channel_id=1, replica_groups=mesh['grp'=4,'tm'=8] {'tm'}, dimensions={0}, use_global_device_ids=true | all-gather | bytes 36864 | tf_op jit(solution)/shard_map/all_gather | solution.py:13
  299.2 14.0 %all-gather.2 = f32[8,1,1024]{2,1,0:T(1,128)S(1)} all-gather(f32[1,1,1024]{2,1,0:T(1,128)S(1)} %slice_bitcast_fusion.1), channel_id=1, replica_groups=mesh['grp'=4,'tm'=8] {'tm'}, dimensions={0}, use_global_device_ids=true | all-gather | bytes 36864 | tf_op jit(solution)/shard_map/all_gather | solution.py:13
  313.6 14.0 %all-gather = f32[8,1,1024]{2,1,0:T(1,128)S(1)} all-gather(f32[1,1,1024]{2,1,0:T(1,128)S(1)} %slice_bitcast_fusion.2), channel_id=1, replica_groups=mesh['grp'=4,'tm'=8] {'tm'}, dimensions={0}, use_global_device_ids=true | all-gather | bytes 36864 | tf_op jit(solution)/shard_map/all_gather | solution.py:13
  328.0 14.2 %all-gather.4 = f32[8,1,1024]{2,1,0:T(1,128)S(1)} all-gather(f32[1,1,1024]{2,1,0:T(1,128)S(1)} %get-tuple-element.572), channel_id=1, replica_groups=mesh['grp'=4,'tm'=8] {'tm'}, dimensions={0}, use_global_device_ids=true | all-gather | bytes 36864 | tf_op jit(solution)/shard_map/all_gather | solution.py:13
  342.3 5.9 %while.33 = (s32[]{:T(128)}, f32[1024]{0:T(1024)S(1)}, f32[1024]{0:T(1024)S(1)}, s32[]{:T(128)}, f32[8,1024]{1,0:T(8,128)S(1)}, /*index=5*/f32[8,1024]{1,0:T(8,1...) while((s32[]{:T(128)}, f32[1024]{0:T(1024)S(1)}, ...), condition=%wide.region_3.4_spmd, body=%wide.region_2.3_spmd.sunk | while | flops 8198 | bytes 65715 | solution.py:22
  348.1 14.0 %all-gather.1 = f32[8,1,1024]{2,1,0:T(1,128)S(1)} all-gather(f32[1,1,1024]{2,1,0:T(1,128)S(1)} %get-tuple-element.573), channel_id=1, replica_groups=mesh['grp'=4,'tm'=8] {'tm'}, dimensions={0}, use_global_device_ids=true | all-gather | bytes 36864 | tf_op jit(solution)/shard_map/all_gather | solution.py:13
  362.2 1.8 subtract_convert_fusion
  366.8 4.2 pad_maximum_fusion
  371.0 9.0 %copy.466 = f32[512,4096]{1,0:T(8,128)} copy(f32[512,4096]{0,1:T(8,128)} %pad_maximum_fusion) | data formatting | bytes 16777216
  384.1 146.1 %reduce-scatter.4.cloned.1.call-done = f32[16,4096]{1,0:T(8,128)} async-done(((f32[512,4096]{1,0:T(8,128)}), f32[16,4096]{1,0:T(8,128)}) %reduce-scatter.4.cloned.1.call-update) | async-done | bytes 262160
  530.2 1.7 fusion.185
  (675 shorter events, 198.2 us)
Async XLA Ops:
  7.2 19.3 %copy-start = (bf16[512,2048]{1,0:T(8,128)(2,1)S(1)}, bf16[512,2048]{1,0:T(8,128)(2,1)}, u32[]{:S(2)}) copy-start(bf16[512,2048]{1,0:T(8,128)(2,1)} %param.17) | copy-start | bytes 6291460
  7.2 523.0 %reduce-scatter.4.cloned.1.call-start = ((), (), s32[]{:S(2)}) async-start(), calls=%async_computation.1 | async-start | bytes 8650752
  12.3 113.7 %copy-start.1 = (f32[8,16,1024]{2,0,1:T(8,128)}, f32[8,16,1024]{2,0,1:T(8,128)S(1)}, u32[]{:S(2)}) copy-start(f32[8,16,1024]{2,0,1:T(8,128)S(1)} %get-tuple-element.768) | copy-start | bytes 1572868
  12.3 113.7 %copy-start.3 = (f32[8,16,1024]{2,0,1:T(8,128)}, f32[8,16,1024]{2,0,1:T(8,128)S(1)}, u32[]{:S(2)}) copy-start(f32[8,16,1024]{2,0,1:T(8,128)S(1)} %get-tuple-element.769) | copy-start | bytes 1572868
  117.0 18.0 %copy-start.119 = (f32[8,1,1024]{2,1,0:T(1,128)S(1)}, f32[8,1,1024]{2,1,0:T(1,128)}, u32[]{:S(2)}) copy-start(f32[8,1,1024]{2,1,0:T(1,128)} %copy-done.118) | copy-start | bytes 98308
  117.0 18.0 %copy-start.125 = (f32[8,1,1024]{2,1,0:T(1,128)S(1)}, f32[8,1,1024]{2,1,0:T(1,128)}, u32[]{:S(2)}) copy-start(f32[8,1,1024]{2,1,0:T(1,128)} %copy-done.124) | copy-start | bytes 98308
  117.0 19.5 %copy-start.115 = (f32[8,1,1024]{2,1,0:T(1,128)S(1)}, f32[8,1,1024]{2,1,0:T(1,128)}, u32[]{:S(2)}) copy-start(f32[8,1,1024]{2,1,0:T(1,128)} %copy-done.114) | copy-start | bytes 98308
  117.1 19.5 %copy-start.121 = (f32[8,1,1024]{2,1,0:T(1,128)S(1)}, f32[8,1,1024]{2,1,0:T(1,128)}, u32[]{:S(2)}) copy-start(f32[8,1,1024]{2,1,0:T(1,128)} %copy-done.120) | copy-start | bytes 98308
  121.2 16.8 %copy-start.117 = (f32[8,1,1024]{2,1,0:T(1,128)S(1)}, f32[8,1,1024]{2,1,0:T(1,128)}, u32[]{:S(2)}) copy-start(f32[8,1,1024]{2,1,0:T(1,128)} %copy-done.116) | copy-start | bytes 98308
  133.6 28.2 %copy-start.158 = (f32[1,1024]{1,0:T(1,128)S(1)}, f32[1,1024]{1,0:T(1,128)}, u32[]{:S(2)}) copy-start(f32[1,1024]{1,0:T(1,128)} %slice.1278) | copy-start | bytes 12292
  139.5 42.8 %copy-start.88 = (f32[8,1,1024]{2,0,1:T(8,128)S(1)}, f32[8,1,1024]{2,0,1:T(8,128)}, u32[]{:S(2)}) copy-start(f32[8,1,1024]{2,0,1:T(8,128)} %get-tuple-element.258) | copy-start | bytes 98308
  139.5 42.8 %copy-start.89 = (f32[8,1,1024]{2,0,1:T(8,128)S(1)}, f32[8,1,1024]{2,0,1:T(8,128)}, u32[]{:S(2)}) copy-start(f32[8,1,1024]{2,0,1:T(8,128)} %get-tuple-element.331) | copy-start | bytes 98308
  150.4 21.4 %copy-start.143 = (f32[3,1024]{1,0:T(4,128)}, f32[3,1024]{1,0:T(4,128)S(1)}, u32[]{:S(2)}) copy-start(f32[3,1024]{1,0:T(4,128)S(1)} %slice.1053) | copy-start | bytes 36868
  171.8 50.4 %copy-start.29 = (f32[8,1,1024]{2,1,0:T(1,128)S(1)}, f32[8,1,1024]{2,1,0:T(1,128)}, u32[]{:S(2)}) copy-start(f32[8,1,1024]{2,1,0:T(1,128)} %copy-done.27) | copy-start | bytes 98308
  171.8 50.4 %copy-start.32 = (f32[8,1,1024]{2,1,0:T(1,128)S(1)}, f32[8,1,1024]{2,1,0:T(1,128)}, u32[]{:S(2)}) copy-start(f32[8,1,1024]{2,1,0:T(1,128)} %copy-done.30) | copy-start | bytes 98308
  179.9 52.1 %copy-start.147 = (f32[8,1,1024]{2,0,1:T(8,128)S(1)}, f32[8,1,1024]{2,0,1:T(8,128)}, u32[]{:S(2)}) copy-start(f32[8,1,1024]{2,0,1:T(8,128)} %get-tuple-element.284) | copy-start | bytes 98308
  182.3 49.7 %copy-start.146 = (f32[8,1,1024]{2,0,1:T(8,128)S(1)}, f32[8,1,1024]{2,0,1:T(8,128)}, u32[]{:S(2)}) copy-start(f32[8,1,1024]{2,0,1:T(8,128)} %get-tuple-element.287) | copy-start | bytes 98308
  182.3 49.7 %copy-start.148 = (f32[8,1024]{1,0:T(8,128)S(1)}, f32[8,1024]{1,0:T(8,128)}, u32[]{:S(2)}) copy-start(f32[8,1024]{1,0:T(8,128)} %rev.19) | copy-start | bytes 98308
  182.3 49.7 %copy-start.149 = (f32[8,1024]{1,0:T(8,128)S(1)}, f32[8,1024]{1,0:T(8,128)}, u32[]{:S(2)}) copy-start(f32[8,1024]{1,0:T(8,128)} %rev.20) | copy-start | bytes 98308
  182.3 49.7 %copy-start.150 = (f32[8,1024]{1,0:T(8,128)S(1)}, f32[8,1024]{1,0:T(8,128)}, u32[]{:S(2)}) copy-start(f32[8,1024]{1,0:T(8,128)} %rev.17) | copy-start | bytes 98308
  182.3 49.7 %copy-start.151 = (f32[8,1024]{1,0:T(8,128)S(1)}, f32[8,1024]{1,0:T(8,128)}, u32[]{:S(2)}) copy-start(f32[8,1024]{1,0:T(8,128)} %rev.18) | copy-start | bytes 98308
  183.8 39.1 %copy-start.33 = (f32[8,16,1024]{2,0,1:T(8,128)S(1)}, f32[8,16,1024]{2,0,1:T(8,128)}, u32[]{:S(2)}) copy-start(f32[8,16,1024]{2,0,1:T(8,128)} %get-tuple-element.711) | copy-start | bytes 1572868
  233.9 35.8 %copy-start.5 = (f32[8,16,1024]{2,1,0:T(8,128)}, f32[8,16,1024]{2,1,0:T(8,128)S(1)}, u32[]{:S(2)}) copy-start(f32[8,16,1024]{2,1,0:T(8,128)S(1)} %copy.460) | copy-start | bytes 1572868
  233.9 35.1 %copy-start.34 = (f32[8,16,1024]{2,0,1:T(8,128)S(1)}, f32[8,16,1024]{2,0,1:T(8,128)}, u32[]{:S(2)}) copy-start(f32[8,16,1024]{2,0,1:T(8,128)} %get-tuple-element.538) | copy-start | bytes 1572868
  233.9 35.1 %copy-start.95 = (f32[8,1,1024]{2,1,0:T(1,128)S(1)}, f32[8,1,1024]{2,1,0:T(1,128)}, u32[]{:S(2)}) copy-start(f32[8,1,1024]{2,1,0:T(1,128)} %copy-done.94) | copy-start | bytes 98308
  233.9 35.0 %copy-start.97 = (f32[8,1,1024]{2,1,0:T(1,128)S(1)}, f32[8,1,1024]{2,1,0:T(1,128)}, u32[]{:S(2)}) copy-start(f32[8,1,1024]{2,1,0:T(1,128)} %copy-done.96) | copy-start | bytes 98308
  234.2 37.3 %copy-start.7 = (f32[8,16,1024]{2,1,0:T(8,128)}, f32[8,16,1024]{2,1,0:T(8,128)S(1)}, u32[]{:S(2)}) copy-start(f32[8,16,1024]{2,1,0:T(8,128)S(1)} %copy.462) | copy-start | bytes 1572868
  284.9 43.1 %copy-start.9 = (f32[8,16,1024]{2,1,0:T(8,128)}, f32[8,16,1024]{2,1,0:T(8,128)S(1)}, u32[]{:S(2)}) copy-start(f32[8,16,1024]{2,1,0:T(8,128)S(1)} %copy.395) | copy-start | bytes 1572868
  299.2 43.0 %copy-start.10 = (f32[8,16,1024]{2,1,0:T(8,128)}, f32[8,16,1024]{2,1,0:T(8,128)S(1)}, u32[]{:S(2)}) copy-start(f32[8,16,1024]{2,1,0:T(8,128)S(1)} %copy.392) | copy-start | bytes 1572868
  313.6 28.6 %copy-start.11 = (f32[8,16,1024]{2,1,0:T(8,128)}, f32[8,16,1024]{2,1,0:T(8,128)S(1)}, u32[]{:S(2)}) copy-start(f32[8,16,1024]{2,1,0:T(8,128)S(1)} %copy.393) | copy-start | bytes 1572868
  342.2 21.9 %copy-start.6 = (f32[8,16,1024]{2,1,0:T(8,128)S(1)}, f32[8,16,1024]{2,1,0:T(8,128)}, u32[]{:S(2)}) copy-start(f32[8,16,1024]{2,1,0:T(8,128)} %copy-done.5) | copy-start | bytes 1572868
  342.2 21.9 %copy-start.8 = (f32[8,16,1024]{2,1,0:T(8,128)S(1)}, f32[8,16,1024]{2,1,0:T(8,128)}, u32[]{:S(2)}) copy-start(f32[8,16,1024]{2,1,0:T(8,128)} %copy-done.7) | copy-start | bytes 1572868
  (134 other events, 854.5 us)
Sparse Core Ops, SparseCore 0:
  380.1 150.0 reduce-scatter.3
where the time goes:
time: 550 us; the launch traced here: 539 us
  local copies, waits for them, and re-layouts  177 us (32%)
  waiting for transfers between devices  146 us (27%)
  blocking collectives  99.9 us (18%)
  other arithmetic  91.5 us (17%)
  between operations  16.9 us (3%)
  matrix products  7.03 us (1%)
    unnamed x2, waiting for transfers between devices  146 us
    all_gather x7, blocking collectives, prefix(): gathered = jax.tree.map(lambda a: lax.all_gather(a, axis), part)  99.9 us
    slice x67, local copies, waits for them, and re-layouts, chain(): inclusive = lax.associative_scan(combine, summary)  80.2 us
    unnamed x406, local copies, waits for them, and re-layouts  66 us
    unnamed x33, other arithmetic  34.7 us
    add x41, other arithmetic, combine(): return (prod_re, prod_im, moved_re + next_re, moved_im + next_im)  18.9 us
  transfers between devices with their start and end apart: 1, of which 1 were waited for; matrix products, arithmetic and copies ran while one was open for 1% of the time, Pallas kernels for 0%

commit v1 on v0

v1 whole, which is shorter than its diff:
```python
import functools

import jax
import jax.numpy as jnp
from jax import lax
from jax.experimental import pallas as pl
from jax.experimental.pallas import tpu as pltpu
from jax.sharding import PartitionSpec as P

MESH = pl.DeviceIdType.MESH
F32 = jnp.float32
BF16 = jnp.bfloat16
SUB = 8
LANE = 128


def cmul(ar, ai, br, bi):
    return ar * br - ai * bi, ar * bi + ai * br


def square_times(re, im, count):
    while count > 1:
        re, im = cmul(re, im, re, im)
        count //= 2
    return re, im


def kernel(
    groups, times,
    sig_ref, damp_ref, par_ref, win_ref, wout_ref, skip_ref, cot_ref,
    mixed_ref, gsig_ref, gin_ref, gout_ref,
    dampb, sigb, cotb, x, y, ends, enters, cmsg, crecv, ldev, cfull,
    fsend, fgat, factor, dsend, dgat, packed, drive, pbuf, zsend, zgat, fsum, osend, ogat,
    csend_sem, crecv_sem, fsend_sem, frecv_sem, dsend_sem, drecv_sem,
    zsend_sem, zrecv_sem, osend_sem, orecv_sem,
):
    steps, feat = sig_ref.shape
    width = par_ref.shape[1]
    inner = steps // SUB
    planes = times // 2
    members = groups * 2
    block = 2 * width // groups
    chunks = block // LANE
    tiles = width // LANE
    own_rows = feat // (groups * times)
    pair_rows = 2 * own_rows

    g = lax.axis_index("grp")
    t = lax.axis_index("tm")
    c = t % 2
    z = t // 2
    me = g * 2 + c

    barrier = pltpu.get_barrier_semaphore()

    def greet_time(d, carry):
        pl.semaphore_signal(barrier, inc=1, device_id=(g, (t + d) % times), device_id_type=MESH)
        return carry

    lax.fori_loop(1, times, greet_time, 0)

    def greet_plane(d, carry):
        pl.semaphore_signal(
            barrier, inc=1, device_id=((g + d // 2) % groups, z * 2 + d % 2), device_id_type=MESH
        )
        return carry

    lax.fori_loop(2, members, greet_plane, 0)

    row = lax.broadcasted_iota(jnp.int32, (steps, steps), 0)
    col = lax.broadcasted_iota(jnp.int32, (steps, steps), 1)
    hit = col == (row % SUB) * inner + row // SUB
    back = row == (col % SUB) * inner + col // SUB
    order = jnp.where(hit, 1.0, 0.0).astype(BF16)
    restore = jnp.where(back, 1.0, 0.0).astype(BF16)
    damp = jnp.sum(jnp.where(hit, damp_ref[...], 0.0), axis=1, keepdims=True)
    dampb[:steps, :] = jnp.broadcast_to(damp, (steps, LANE))
    sig = jnp.dot(order, sig_ref[...], preferred_element_type=F32)
    cot = jnp.dot(order, cot_ref[...], preferred_element_type=F32)
    sigb[...] = sig.astype(BF16)
    cotb[...] = cot.astype(BF16)
    fsend[0] = sig.T
    fsend[1] = cot.T

    pl.semaphore_wait(barrier, (times - 1) + (members - 2))

    def factor_copy(d):
        m = (me + d) % members
        return pltpu.make_async_remote_copy(
            src_ref=fsend.at[m % 2], dst_ref=fgat.at[me],
            send_sem=fsend_sem.at[d], recv_sem=frecv_sem.at[d],
            device_id=(m // 2, z * 2 + m % 2), device_id_type=MESH,
        )

    def start_factor(d, carry):
        factor_copy(d).start()
        return carry

    lax.fori_loop(1, members, start_factor, 0)
    fgat[me] = fsend[c]

    gamma = par_ref[2:3, :]
    x[:, :width] = gamma * jnp.dot(sigb[...], win_ref[:, :width], preferred_element_type=F32)
    x[:, width:] = gamma * jnp.dot(sigb[...], win_ref[:, width:], preferred_element_type=F32)
    y[...] = jnp.dot(cotb[...], wout_ref[...], preferred_element_type=F32)

    lre = jnp.broadcast_to(par_ref[0:1, :], (SUB, width))
    lim = jnp.broadcast_to(par_ref[1:2, :], (SUB, width))

    def rows_of(j):
        return slice(j * SUB, (j + 1) * SUB)

    def forward_step(j, sre, sim):
        rows = rows_of(j)
        a = dampb[rows, 0:1]
        mre, mim = cmul(lre, lim, sre, sim)
        return a * mre + x[rows, :width], a * mim + x[rows, width:]

    def backward_step(j, bre, bim):
        rows = rows_of(j)
        a = dampb[rows, 0:1]
        are = y[rows, :width] + bre
        aim = y[rows, width:] + bim
        return are, aim, a * (lre * are + lim * aim), a * (lre * aim - lim * are)

    zero = jnp.zeros((SUB, width), F32)
    sre, sim = zero, zero
    for j in range(inner):
        sre, sim = forward_step(j, sre, sim)
    ends[0] = sre
    ends[1] = sim
    bre, bim = zero, zero
    for j in reversed(range(inner)):
        _, _, bre, bim = backward_step(j, bre, bim)
    ends[2] = bre
    ends[3] = bim
    prod = dampb[0:SUB, :]
    for j in range(1, inner):
        prod = prod * dampb[rows_of(j), :]
    dampb[steps : steps + SUB, :] = prod

    one_re, one_im = square_times(par_ref[0:1, :], par_ref[1:2, :], inner)
    place = lax.broadcasted_iota(jnp.int32, (SUB, width), 0)

    def edge_power(index):
        pre, pim = jnp.ones((SUB, width), F32), zero
        qre, qim = one_re, one_im
        bit = 1
        while bit < SUB:
            on = (index // bit) % 2 == 1
            pre, pim = cmul(pre, pim, jnp.where(on, qre, 1.0), jnp.where(on, qim, 0.0))
            qre, qim = cmul(qre, qim, qre, qim)
            bit *= 2
        return pre, pim, qre, qim

    pre, pim, dre, dim = edge_power(place)
    tre, tim, _, _ = edge_power(SUB - 1 - place)

    ere = eim = jnp.zeros((1, width), F32)
    total = jnp.ones((1, LANE), F32)
    for o in range(SUB):
        one = slice(o, o + 1)
        enters[0, one] = ere
        enters[1, one] = eim
        dampb[steps + SUB + o : steps + SUB + o + 1, :] = total
        here = dampb[steps + o : steps + o + 1, :]
        mre, mim = cmul(one_re, one_im, ere, eim)
        ere = here[:, 0:1] * mre + ends[0, one]
        eim = here[:, 0:1] * mim + ends[1, one]
        total = total * here
    ore = oim = jnp.zeros((1, width), F32)
    tail = jnp.ones((1, LANE), F32)
    for o in reversed(range(SUB)):
        one = slice(o, o + 1)
        enters[2, one] = ore
        enters[3, one] = oim
        dampb[steps + 2 * SUB + o : steps + 2 * SUB + o + 1, :] = tail
        here = dampb[steps + o : steps + o + 1, :]
        mre = one_re * ore + one_im * oim
        mim = one_re * oim - one_im * ore
        ore = here[:, 0:1] * mre + ends[2, one]
        oim = here[:, 0:1] * mim + ends[3, one]
        tail = tail * here

    for i in range(tiles):
        lanes = slice(i * LANE, (i + 1) * LANE)
        one = slice(i, i + 1)
        cmsg[0, 0, one] = ere[:, lanes]
        cmsg[0, 1, one] = eim[:, lanes]
        cmsg[1, 0, one] = ore[:, lanes]
        cmsg[1, 1, one] = oim[:, lanes]
        ldev[0, one] = dre[:, lanes]
        ldev[1, one] = dim[:, lanes]
    cmsg[0, 2] = jnp.broadcast_to(total, (tiles, LANE))
    cmsg[1, 2] = jnp.broadcast_to(total, (tiles, LANE))

    def carry_copy(q):
        later = jnp.where(q > t, 0, 1)
        return pltpu.make_async_remote_copy(
            src_ref=cmsg.at[later], dst_ref=crecv.at[t],
            send_sem=csend_sem.at[q], recv_sem=crecv_sem.at[t],
            device_id=(g, q), device_id_type=MESH,
        )

    def carry_arrival(q):
        return pltpu.make_async_remote_copy(
            src_ref=cmsg.at[0], dst_ref=crecv.at[q],
            send_sem=csend_sem.at[q], recv_sem=crecv_sem.at[q],
            device_id=(g, q), device_id_type=MESH,
        )

    def start_carry(d, carry):
        carry_copy((t + d) % times).start()
        return carry

    lax.fori_loop(1, times, start_carry, 0)

    def ahead(q, carry):
        carry_arrival(q).wait_recv()
        mre, mim = cmul(ldev[0], ldev[1], carry[0], carry[1])
        factor_q = crecv[q, 2]
        return factor_q * mre + crecv[q, 0], factor_q * mim + crecv[q, 1]

    def behind(i, carry):
        q = times - 1 - i
        carry_arrival(q).wait_recv()
        mre = ldev[0] * carry[0] + ldev[1] * carry[1]
        mim = ldev[0] * carry[1] - ldev[1] * carry[0]
        factor_q = crecv[q, 2]
        return factor_q * mre + crecv[q, 0], factor_q * mim + crecv[q, 1]

    none = jnp.zeros((tiles, LANE), F32)
    cfull[0], cfull[1] = lax.fori_loop(0, t, ahead, (none, none))
    cfull[2], cfull[3] = lax.fori_loop(0, times - 1 - t, behind, (none, none))

    def wide(i):
        return jnp.concatenate([cfull[i, k : k + 1, :] for k in range(tiles)], axis=1)

    def rounded(value):
        return value.astype(BF16).astype(F32)

    mre, mim = cmul(pre, pim, wide(0), wide(1))
    reach = dampb[steps + SUB : steps + 2 * SUB, 0:1]
    sre = enters[0] + reach * mre
    sim = enters[1] + reach * mim
    for j in range(inner):
        sre, sim = forward_step(j, sre, sim)
        kre, kim = rounded(sre), rounded(sim)
        for i in range(tiles):
            lanes = slice(i * LANE, (i + 1) * LANE)
            dsend[1, i, rows_of(j)] = kre[:, lanes]
            dsend[1, tiles + i, rows_of(j)] = kim[:, lanes]

    kre, kim = wide(2), wide(3)
    mre = tre * kre + tim * kim
    mim = tre * kim - tim * kre
    reach = dampb[steps + 2 * SUB : steps + 3 * SUB, 0:1]
    bre = enters[2] + reach * mre
    bim = enters[3] + reach * mim
    for j in reversed(range(inner)):
        are, aim, bre, bim = backward_step(j, bre, bim)
        kre, kim = rounded(gamma * are), rounded(gamma * aim)
        for i in range(tiles):
            lanes = slice(i * LANE, (i + 1) * LANE)
            dsend[0, i, rows_of(j)] = kre[:, lanes]
            dsend[0, tiles + i, rows_of(j)] = kim[:, lanes]

    def drive_copy(k, d):
        m = (me + d) % members
        return pltpu.make_async_remote_copy(
            src_ref=dsend.at[m % 2, (m // 2) * chunks + k], dst_ref=dgat.at[k, me],
            send_sem=dsend_sem.at[k, d], recv_sem=drecv_sem.at[k, d],
            device_id=(m // 2, z * 2 + m % 2), device_id_type=MESH,
        )

    for k in range(chunks):
        def start_drive(d, carry, k=k):
            drive_copy(k, d).start()
            return carry

        lax.fori_loop(1, members, start_drive, 0)

    for k in range(chunks):
        dgat[k, me] = dsend[c, g * chunks + k]

    for i in range(2 * tiles):
        lanes = slice(i * LANE, (i + 1) * LANE)
        packed[:, lanes] = dsend[1, i].astype(BF16)
        drive[:, lanes] = dsend[0, i].astype(BF16)

    turned = (((1,), (1,)), ((), ()))
    out = lax.dot_general(packed[...], wout_ref[...], turned, preferred_element_type=F32)
    out = (out + skip_ref[...] * sigb[...].astype(F32)).astype(BF16)
    mixed_ref[...] = jnp.dot(restore, out, preferred_element_type=F32).astype(BF16)
    out = lax.dot_general(drive[...], win_ref[...], turned, preferred_element_type=F32)
    out = (out + skip_ref[...] * cotb[...].astype(F32)).astype(BF16)
    gsig_ref[...] = jnp.dot(restore, out, preferred_element_type=F32).astype(BF16)

    def await_factor(d, carry):
        factor_copy(d).wait_recv()
        return carry

    lax.fori_loop(1, members, await_factor, 0)
    for m in range(members):
        factor[:, m * steps : (m + 1) * steps] = fgat[m].astype(BF16)

    def plane_copy(k, d):
        other = (z + d) % planes
        return pltpu.make_async_remote_copy(
            src_ref=zsend.at[k, other], dst_ref=zgat.at[k, z],
            send_sem=zsend_sem.at[k, d], recv_sem=zrecv_sem.at[k, d],
            device_id=(g, other * 2 + c), device_id_type=MESH,
        )

    for k in range(chunks):
        def await_drive(d, carry, k=k):
            drive_copy(k, d).wait_recv()
            return carry

        lax.fori_loop(1, members, await_drive, 0)
        whole = dgat[k].reshape(members * steps, LANE).astype(BF16)
        pbuf[k] = jnp.dot(factor[...], whole, preferred_element_type=F32)
        for gg in range(groups):
            for zz in range(planes):
                first = gg * times * own_rows + zz * pair_rows
                zsend[k, zz, gg * pair_rows : (gg + 1) * pair_rows] = pbuf[k, first : first + pair_rows]

        def start_plane(d, carry, k=k):
            plane_copy(k, d).start()
            return carry

        lax.fori_loop(1, planes, start_plane, 0)

    for k in range(chunks):
        def add_plane(d, acc, k=k):
            plane_copy(k, d).wait_recv()
            return acc + zgat[k, (z + planes - d) % planes]

        fsum[:, k * LANE : (k + 1) * LANE] = lax.fori_loop(1, planes, add_plane, zsend[k, z])

    for m in range(members):
        osend[m] = fsum[m * own_rows : (m + 1) * own_rows, :]

    def owner_copy(d):
        m = (me + d) % members
        return pltpu.make_async_remote_copy(
            src_ref=osend.at[m], dst_ref=ogat.at[me],
            send_sem=osend_sem.at[d], recv_sem=orecv_sem.at[d],
            device_id=(m // 2, z * 2 + m % 2), device_id_type=MESH,
        )

    def start_owner(d, carry):
        owner_copy(d).start()
        return carry

    lax.fori_loop(1, members, start_owner, 0)
    ogat[me] = osend[me]

    def await_owner(d, carry):
        owner_copy(d).wait_recv()
        return carry

    lax.fori_loop(1, members, await_owner, 0)
    for gg in range(groups):
        lanes = slice(gg * block, (gg + 1) * block)
        gin_ref[:, lanes] = ogat[gg * 2]
        gout_ref[:, lanes] = ogat[gg * 2 + 1]

    def drain_members(d, carry):
        factor_copy(d).wait_send()
        owner_copy(d).wait_send()
        for k in range(chunks):
            drive_copy(k, d).wait_send()
        return carry

    lax.fori_loop(1, members, drain_members, 0)

    def drain_planes(d, carry):
        for k in range(chunks):
            plane_copy(k, d).wait_send()
        return carry

    lax.fori_loop(1, planes, drain_planes, 0)

    def drain_times(d, carry):
        carry_copy((t + d) % times).wait_send()
        return carry

    lax.fori_loop(1, times, drain_times, 0)


def body(groups, times, signal, damping, nu_log, theta, in_weight, out_weight, skip_gain, cotangent):
    _, steps, feat = signal.shape
    width = nu_log.shape[0]
    rate = jnp.exp(nu_log)
    magnitude = jnp.exp(-rate)
    scaling = jnp.sqrt(-jnp.expm1(-2.0 * rate))
    par = jnp.stack([magnitude * jnp.cos(theta), magnitude * jnp.sin(theta), scaling], 0)
    members = groups * 2
    planes = times // 2
    block = 2 * width // groups
    chunks = block // LANE
    tiles = width // LANE
    own_rows = feat // (groups * times)
    plane_rows = feat // planes
    vmem = pl.BlockSpec(memory_space=pltpu.VMEM)
    dma = pltpu.SemaphoreType.DMA
    scratch = [
        pltpu.VMEM((steps + 3 * SUB, LANE), F32),
        pltpu.VMEM((steps, feat), BF16),
        pltpu.VMEM((steps, feat), BF16),
        pltpu.VMEM((steps, 2 * width), F32),
        pltpu.VMEM((steps, 2 * width), F32),
        pltpu.VMEM((4, SUB, width), F32),
        pltpu.VMEM((4, SUB, width), F32),
        pltpu.VMEM((2, 3, tiles, LANE), F32),
        pltpu.VMEM((times, 3, tiles, LANE), F32),
        pltpu.VMEM((2, tiles, LANE), F32),
        pltpu.VMEM((4, tiles, LANE), F32),
        pltpu.VMEM((2, feat, steps), F32),
        pltpu.VMEM((members, feat, steps), F32),
        pltpu.VMEM((feat, members * steps), BF16),
        pltpu.VMEM((2, 2 * tiles, steps, LANE), F32),
        pltpu.VMEM((chunks, members, steps, LANE), F32),
        pltpu.VMEM((steps, 2 * width), BF16),
        pltpu.VMEM((steps, 2 * width), BF16),
        pltpu.VMEM((chunks, feat, LANE), F32),
        pltpu.VMEM((chunks, planes, plane_rows, LANE), F32),
        pltpu.VMEM((chunks, planes, plane_rows, LANE), F32),
        pltpu.VMEM((plane_rows, block), F32),
        pltpu.VMEM((members, own_rows, block), F32),
        pltpu.VMEM((members, own_rows, block), F32),
        dma((times,)), dma((times,)),
        dma((members,)), dma((members,)),
        dma((chunks, members)), dma((chunks, members)),
        dma((chunks, planes)), dma((chunks, planes)),
        dma((members,)), dma((members,)),
    ]
    out = pl.pallas_call(
        functools.partial(kernel, groups, times),
        out_shape=(
            jax.ShapeDtypeStruct((steps, feat), BF16),
            jax.ShapeDtypeStruct((steps, feat), BF16),
            jax.ShapeDtypeStruct((own_rows, 2 * width), F32),
            jax.ShapeDtypeStruct((own_rows, 2 * width), F32),
        ),
        in_specs=[vmem] * 7,
        out_specs=(vmem,) * 4,
        scratch_shapes=scratch,
        compiler_params=pltpu.CompilerParams(
            collective_id=0, has_side_effects=True, vmem_limit_bytes=48 * 1024 * 1024
        ),
        cost_estimate=pl.CostEstimate(
            flops=14 * steps * feat * 2 * width, bytes_accessed=8 * feat * width, transcendentals=0
        ),
    )(signal[0], damping, par, in_weight, out_weight, skip_gain[None], cotangent[0])
    return (out[0][None], out[1][None], out[2], out[3])


def solution(mesh):
    placed = (P("grp", "tm", None), P("grp", "tm"), P(), P(), P(), P(), P(), P("grp", "tm", None))
    return jax.shard_map(
        functools.partial(body, mesh.shape["grp"], mesh.shape["tm"]),
        mesh=mesh,
        in_specs=placed,
        out_specs=(
            P("grp", "tm", None),
            P("grp", "tm", None),
            P(("grp", "tm"), None),
            P(("grp", "tm"), None),
        ),
        check_vma=False,
    )
```

time: 550 us -> 75.8 us (0.14); the launches traced: 539 us -> 75.5 us
  local copies, waits for them, and re-layouts: 177 us -> 8.94 us
  waiting for transfers between devices: 146 us -> 0 us
  blocking collectives: 99.9 us -> 0 us
  other arithmetic: 91.5 us -> 0.76 us
  Pallas kernels: 0 us -> 65.1 us
  between operations: 16.9 us -> 0.66 us
  matrix products: 7.03 us -> 0 us
    unnamed x2 -> x0, waiting for transfers between devices: 146 us -> none
    all_gather x7 -> x0, blocking collectives: 99.9 us -> none  [prefix(): gathered = jax.tree.map(lambda a: lax.all_gather(a, axis), part)]
    slice x84 -> x0, local copies, waits for them, and re-layouts: 85.4 us -> none  [the longest x67 80.2 us: chain(): inclusive = lax.associative_scan(combine, summary)]
    pallas_call x0 -> x1, Pallas kernels: none -> 65.1 us  [body(): pl.pallas_call(functools.partial(kernel, groups, times), out_shape=(jax.S...]
    unnamed x406 -> x16, local copies, waits for them, and re-layouts: 66 us -> 8.94 us
    unnamed x33 -> x0, other arithmetic: 34.7 us -> none
    add x69 -> x0, other arithmetic: 31.3 us -> none  [the longest x41 18.9 us: combine(): return (prod_re, prod_im, moved_re + next_re, moved_im + next_im)]
    concatenate x17 -> x0, other arithmetic: 14.1 us -> none  [the longest x16 9.9 us: chain(): inclusive = lax.associative_scan(combine, summary)]
  transfers between devices with their start and end apart: 1 -> 0, of which waited for: 1 -> 0; matrix products, arithmetic and copies ran while one was open for 1% -> 0% of each run, Pallas kernels for 0% -> 0%
where the time goes in v1:
time: 75.8 us; the launch traced here: 75.5 us
  Pallas kernels  65.1 us (86%)
  local copies, waits for them, and re-layouts  8.94 us (12%)
  other arithmetic  0.76 us (1%)
    pallas_call x1, Pallas kernels, body(): pl.pallas_call(functools.partial(kernel, groups, times), out_shape=(jax.S...  65.1 us
    unnamed x16, local copies, waits for them, and re-layouts  8.94 us

profile of v1, /device:TPU:0, one launch (start us, length us, event | category | flops | bytes accessed | tf_op | source)
XLA Modules:
  0.0 75.5 jit_solution(3919819193452239205)
XLA Ops:
  0.6 0.7 cosine_multiply_fusion
  1.4 0.0 copy-start
  1.4 1.6 %copy-done = bf16[512,2048]{1,0:T(8,128)(2,1)S(1)} copy-done((bf16[512,2048]{1,0:T(8,128)(2,1)S(1)}, bf16[512,2048]{1,0:T(8,128)(2,1)}, u32[]{:S(2)}) %copy-start) | copy-done | bytes 2097176
  3.0 0.0 copy-start.1
  3.0 1.6 %copy-done.1 = bf16[512,2048]{1,0:T(8,128)(2,1)S(1)} copy-done((bf16[512,2048]{1,0:T(8,128)(2,1)S(1)}, bf16[512,2048]{1,0:T(8,128)(2,1)}, u32[]{:S(2)}) %copy-start.1) | copy-done | bytes 2097176
  4.6 0.0 copy-start.2
  4.6 0.9 %copy-done.2 = bf16[1,128,512]{2,1,0:T(8,128)(2,1)S(1)} copy-done((bf16[1,128,512]{2,1,0:T(8,128)(2,1)S(1)}, bf16[1,128,512]{2,1,0:T(8,128)(2,1)}, u32[]{:S(2)}) %copy-start.2) | copy-done | bytes 131096
  5.5 0.0 copy-start.3
  5.5 0.9 %copy-done.3 = bf16[1,128,512]{2,1,0:T(8,128)(2,1)S(1)} copy-done((bf16[1,128,512]{2,1,0:T(8,128)(2,1)S(1)}, bf16[1,128,512]{2,1,0:T(8,128)(2,1)}, u32[]{:S(2)}) %copy-start.3) | copy-done | bytes 131096
  6.4 0.0 copy-start.4
  6.4 0.7 copy-done.4
  7.1 0.0 copy-start.5
  7.1 0.7 copy-done.5
  7.7 65.1 %shard_map.111 = (bf16[128,512]{1,0:T(8,128)(2,1)S(1)}, bf16[128,512]{1,0:T(8,128)(2,1)S(1)}, f32[16,2048]{1,0:T(8,128)S(1)}, f32[16,2048]{1,0:T(8,128)S(1)}) custom-call(bf16[128,512]{1,0:T(8,128)(2,1)S(1)} %bitcast.10, f32[1,128]{1,0:T(1,128)S(1)} %copy-done.5, f32[3,1024]{1,0:T(4,128)S(1)} %pad_maximum_fusion.par_ref, bf16[512,2048]{1,0:T(8,128)(2,1)S(1)} %copy-done, ...), custom_call_target="tpu_custom_call" | custom-call | flops 1879048192 | bytes 4194304 | tf_op jit(solution)/shard_map/pallas_call | solution.py:439
  72.9 0.7 copy.16
  73.6 0.7 copy.17
  74.2 0.7 copy.18
  74.9 0.7 copy.19
  (1 shorter events, 0.0 us)
Async XLA Ops:
  1.4 1.6 %copy-start = (bf16[512,2048]{1,0:T(8,128)(2,1)S(1)}, bf16[512,2048]{1,0:T(8,128)(2,1)}, u32[]{:S(2)}) copy-start(bf16[512,2048]{1,0:T(8,128)(2,1)} %win_ref.1) | copy-start | bytes 6291460
  3.0 1.6 %copy-start.1 = (bf16[512,2048]{1,0:T(8,128)(2,1)S(1)}, bf16[512,2048]{1,0:T(8,128)(2,1)}, u32[]{:S(2)}) copy-start(bf16[512,2048]{1,0:T(8,128)(2,1)} %wout_ref.1) | copy-start | bytes 6291460
  4.6 0.9 %copy-start.2 = (bf16[1,128,512]{2,1,0:T(8,128)(2,1)S(1)}, bf16[1,128,512]{2,1,0:T(8,128)(2,1)}, u32[]{:S(2)}) copy-start(bf16[1,128,512]{2,1,0:T(8,128)(2,1)} %param.8) | copy-start | bytes 393220
  5.5 0.9 %copy-start.3 = (bf16[1,128,512]{2,1,0:T(8,128)(2,1)S(1)}, bf16[1,128,512]{2,1,0:T(8,128)(2,1)}, u32[]{:S(2)}) copy-start(bf16[1,128,512]{2,1,0:T(8,128)(2,1)} %param.15) | copy-start | bytes 393220
  6.4 0.7 copy-start.4
  7.1 0.7 copy-start.5

commit v2 on v1

--- a/solution.py
+++ b/solution.py
@@ -27,14 +27,15 @@
 
 def kernel(
     groups, times,
-    sig_ref, damp_ref, par_ref, win_ref, wout_ref, skip_ref, cot_ref,
+    sig_hbm, damp_hbm, par_ref, win_hbm, wout_hbm, skip_hbm, cot_hbm,
     mixed_ref, gsig_ref, gin_ref, gout_ref,
+    sig_ref, damp_ref, win_ref, wout_ref, skip_ref, cot_ref, load_sem,
     dampb, sigb, cotb, x, y, ends, enters, cmsg, crecv, ldev, cfull,
-    fsend, fgat, factor, dsend, dgat, packed, drive, pbuf, zsend, zgat, fsum, osend, ogat,
+    fsend, fgat, factor, dsend, dgat, packed, drive, pbuf, rsend, rgat, zsend, zgat, osend, ogat,
     csend_sem, crecv_sem, fsend_sem, frecv_sem, dsend_sem, drecv_sem,
-    zsend_sem, zrecv_sem, osend_sem, orecv_sem,
+    rsend_sem, rrecv_sem, zsend_sem, zrecv_sem, osend_sem, orecv_sem,
 ):
-    steps, feat = sig_ref.shape
+    steps, feat = sig_hbm.shape
     width = par_ref.shape[1]
     inner = steps // SUB
     planes = times // 2
@@ -44,6 +45,7 @@
     tiles = width // LANE
     own_rows = feat // (groups * times)
     pair_rows = 2 * own_rows
+    units = 2 * chunks
 
     g = lax.axis_index("grp")
     t = lax.axis_index("tm")
@@ -51,6 +53,21 @@
     z = t // 2
     me = g * 2 + c
 
+    hi = g // 2
+    lo = g % 2
+
+    loads = [
+        pltpu.make_async_copy(src, dst, load_sem.at[i])
+        for i, (src, dst) in enumerate(
+            (
+                (sig_hbm, sig_ref), (cot_hbm, cot_ref), (damp_hbm, damp_ref),
+                (win_hbm, win_ref), (wout_hbm, wout_ref), (skip_hbm, skip_ref),
+            )
+        )
+    ]
+    for load in loads:
+        load.start()
+
     barrier = pltpu.get_barrier_semaphore()
 
     def greet_time(d, carry):
@@ -66,6 +83,9 @@
         return carry
 
     lax.fori_loop(2, members, greet_plane, 0)
+
+    for load in loads[:3]:
+        load.wait()
 
     row = lax.broadcasted_iota(jnp.int32, (steps, steps), 0)
     col = lax.broadcasted_iota(jnp.int32, (steps, steps), 1)
@@ -84,21 +104,34 @@
 
     pl.semaphore_wait(barrier, (times - 1) + (members - 2))
 
+    def place_of(kind):
+        return jnp.where(kind == 0, lo, hi)
+
+    def flipped(device, kind):
+        return jnp.where(kind == 0, (device + 2) % groups, device + 1 - 2 * (device % 2))
+
+    def pair_target(d):
+        kind = c if d == 0 else 1 - c
+        mine = place_of(kind)
+        theirs = mine if d == 1 else 1 - mine
+        device = jnp.where(kind == 0, hi * 2 + theirs, theirs * 2 + lo)
+        return kind, device, mine * 2 + c
+
     def factor_copy(d):
-        m = (me + d) % members
-        return pltpu.make_async_remote_copy(
-            src_ref=fsend.at[m % 2], dst_ref=fgat.at[me],
+        kind, device, slot = pair_target(d)
+        return pltpu.make_async_remote_copy(
+            src_ref=fsend.at[kind], dst_ref=fgat.at[slot],
             send_sem=fsend_sem.at[d], recv_sem=frecv_sem.at[d],
-            device_id=(m // 2, z * 2 + m % 2), device_id_type=MESH,
-        )
-
-    def start_factor(d, carry):
+            device_id=(device, z * 2 + kind), device_id_type=MESH,
+        )
+
+    for d in (0, 2, 1):
         factor_copy(d).start()
-        return carry
-
-    lax.fori_loop(1, members, start_factor, 0)
-    fgat[me] = fsend[c]
-
+    own_slot = place_of(c) * 2 + c
+    fgat[own_slot] = fsend[c]
+
+    for load in loads[3:]:
+        load.wait()
     gamma = par_ref[2:3, :]
     x[:, :width] = gamma * jnp.dot(sigb[...], win_ref[:, :width], preferred_element_type=F32)
     x[:, width:] = gamma * jnp.dot(sigb[...], win_ref[:, width:], preferred_element_type=F32)
@@ -251,6 +284,32 @@
             dsend[1, i, rows_of(j)] = kre[:, lanes]
             dsend[1, tiles + i, rows_of(j)] = kim[:, lanes]
 
+    def unit_column(u, device, kind):
+        keeper = device if u % 2 else flipped(device, kind)
+        return keeper * chunks + u // 2
+
+    def drive_copy(u, d):
+        kind, device, slot = pair_target(d)
+        return pltpu.make_async_remote_copy(
+            src_ref=dsend.at[kind, unit_column(u, device, kind)], dst_ref=dgat.at[u, slot],
+            send_sem=dsend_sem.at[u, d], recv_sem=drecv_sem.at[u, d],
+            device_id=(device, z * 2 + kind), device_id_type=MESH,
+        )
+
+    def start_drive(kind):
+        @pl.when(c == kind)
+        def _():
+            for u in range(units):
+                drive_copy(u, 0).start()
+
+        @pl.when(c != kind)
+        def _():
+            for u in range(units):
+                drive_copy(u, 2).start()
+                drive_copy(u, 1).start()
+
+    start_drive(1)
+
     kre, kim = wide(2), wide(3)
     mre = tre * kre + tim * kim
     mim = tre * kim - tim * kre
@@ -265,23 +324,9 @@
             dsend[0, i, rows_of(j)] = kre[:, lanes]
             dsend[0, tiles + i, rows_of(j)] = kim[:, lanes]
 
-    def drive_copy(k, d):
-        m = (me + d) % members
-        return pltpu.make_async_remote_copy(
-            src_ref=dsend.at[m % 2, (m // 2) * chunks + k], dst_ref=dgat.at[k, me],
-            send_sem=dsend_sem.at[k, d], recv_sem=drecv_sem.at[k, d],
-            device_id=(m // 2, z * 2 + m % 2), device_id_type=MESH,
-        )
-
-    for k in range(chunks):
-        def start_drive(d, carry, k=k):
-            drive_copy(k, d).start()
-            return carry
-
-        lax.fori_loop(1, members, start_drive, 0)
-
-    for k in range(chunks):
-        dgat[k, me] = dsend[c, g * chunks + k]
+    start_drive(0)
+    for u in range(units):
+        dgat[u, own_slot] = dsend[c, unit_column(u, g, c)]
 
     for i in range(2 * tiles):
         lanes = slice(i * LANE, (i + 1) * LANE)
@@ -296,13 +341,17 @@
     out = (out + skip_ref[...] * cotb[...].astype(F32)).astype(BF16)
     gsig_ref[...] = jnp.dot(restore, out, preferred_element_type=F32).astype(BF16)
 
-    def await_factor(d, carry):
+    for d in range(3):
         factor_copy(d).wait_recv()
-        return carry
-
-    lax.fori_loop(1, members, await_factor, 0)
-    for m in range(members):
+    for m in range(4):
         factor[:, m * steps : (m + 1) * steps] = fgat[m].astype(BF16)
+
+    def partner_copy(k):
+        return pltpu.make_async_remote_copy(
+            src_ref=rsend.at[k], dst_ref=rgat.at[k],
+            send_sem=rsend_sem.at[k], recv_sem=rrecv_sem.at[k],
+            device_id=(flipped(g, c), t), device_id_type=MESH,
+        )
 
     def plane_copy(k, d):
         other = (z + d) % planes
@@ -312,65 +361,86 @@
             device_id=(g, other * 2 + c), device_id_type=MESH,
         )
 
-    for k in range(chunks):
-        def await_drive(d, carry, k=k):
-            drive_copy(k, d).wait_recv()
-            return carry
-
-        lax.fori_loop(1, members, await_drive, 0)
-        whole = dgat[k].reshape(members * steps, LANE).astype(BF16)
-        pbuf[k] = jnp.dot(factor[...], whole, preferred_element_type=F32)
+    def owner_copy(k, d):
+        m = (me + d) % members
+        return pltpu.make_async_remote_copy(
+            src_ref=osend.at[k, m], dst_ref=ogat.at[k, me],
+            send_sem=osend_sem.at[k, d], recv_sem=orecv_sem.at[k, d],
+            device_id=(m // 2, z * 2 + m % 2), device_id_type=MESH,
+        )
+
+    def product(u):
+        for d in range(3):
+            drive_copy(u, d).wait_recv()
+        whole = dgat[u].reshape(4 * steps, LANE).astype(BF16)
+        return jnp.dot(factor[...], whole, preferred_element_type=F32)
+
+    def multiply(k):
+        rsend[k] = product(2 * k)
+        partner_copy(k).start()
+        pbuf[k] = product(2 * k + 1)
+
+    def add_partner(k):
+        partner_copy(k).wait_recv()
         for gg in range(groups):
             for zz in range(planes):
                 first = gg * times * own_rows + zz * pair_rows
-                zsend[k, zz, gg * pair_rows : (gg + 1) * pair_rows] = pbuf[k, first : first + pair_rows]
-
-        def start_plane(d, carry, k=k):
+                rows = slice(first, first + pair_rows)
+                zsend[k, zz, gg * pair_rows : (gg + 1) * pair_rows] = pbuf[k, rows] + rgat[k, rows]
+
+        def start_plane(d, carry):
             plane_copy(k, d).start()
             return carry
 
         lax.fori_loop(1, planes, start_plane, 0)
 
-    for k in range(chunks):
-        def add_plane(d, acc, k=k):
+    def add_planes(k):
+        def add_plane(d, acc):
             plane_copy(k, d).wait_recv()
             return acc + zgat[k, (z + planes - d) % planes]
 
-        fsum[:, k * LANE : (k + 1) * LANE] = lax.fori_loop(1, planes, add_plane, zsend[k, z])
-
-    for m in range(members):
-        osend[m] = fsum[m * own_rows : (m + 1) * own_rows, :]
-
-    def owner_copy(d):
-        m = (me + d) % members
-        return pltpu.make_async_remote_copy(
-            src_ref=osend.at[m], dst_ref=ogat.at[me],
-            send_sem=osend_sem.at[d], recv_sem=orecv_sem.at[d],
-            device_id=(m // 2, z * 2 + m % 2), device_id_type=MESH,
-        )
-
-    def start_owner(d, carry):
-        owner_copy(d).start()
-        return carry
-
-    lax.fori_loop(1, members, start_owner, 0)
-    ogat[me] = osend[me]
-
-    def await_owner(d, carry):
-        owner_copy(d).wait_recv()
-        return carry
-
-    lax.fori_loop(1, members, await_owner, 0)
-    for gg in range(groups):
-        lanes = slice(gg * block, (gg + 1) * block)
-        gin_ref[:, lanes] = ogat[gg * 2]
-        gout_ref[:, lanes] = ogat[gg * 2 + 1]
+        pbuf[k, : members * own_rows] = lax.fori_loop(1, planes, add_plane, zsend[k, z])
+        for m in range(members):
+            osend[k, m] = pbuf[k, m * own_rows : (m + 1) * own_rows]
+
+        def start_owner(d, carry):
+            owner_copy(k, d).start()
+            return carry
+
+        lax.fori_loop(1, members, start_owner, 0)
+        ogat[k, me] = osend[k, me]
+
+    def finish(k):
+        def await_owner(d, carry):
+            owner_copy(k, d).wait_recv()
+            return carry
+
+        lax.fori_loop(1, members, await_owner, 0)
+        for gg in range(groups):
+            lanes = slice((gg * chunks + k) * LANE, (gg * chunks + k + 1) * LANE)
+            gin_ref[:, lanes] = ogat[k, gg * 2]
+            gout_ref[:, lanes] = ogat[k, gg * 2 + 1]
+
+    for s in range(chunks + 4):
+        if s < chunks:
+            multiply(s)
+        if 0 <= s - 1 < chunks:
+            add_partner(s - 1)
+        if 0 <= s - 3 < chunks:
+            add_planes(s - 3)
+        if 0 <= s - 4 < chunks:
+            finish(s - 4)
+
+    for d in range(3):
+        factor_copy(d).wait_send()
+        for u in range(units):
+            drive_copy(u, d).wait_send()
+    for k in range(chunks):
+        partner_copy(k).wait_send()
 
     def drain_members(d, carry):
-        factor_copy(d).wait_send()
-        owner_copy(d).wait_send()
         for k in range(chunks):
-            drive_copy(k, d).wait_send()
+            owner_copy(k, d).wait_send()
         return carry
 
     lax.fori_loop(1, members, drain_members, 0)
@@ -406,6 +476,13 @@
     vmem = pl.BlockSpec(memory_space=pltpu.VMEM)
     dma = pltpu.SemaphoreType.DMA
     scratch = [
+        pltpu.VMEM((steps, feat), BF16),
+        pltpu.VMEM((1, steps), F32),
+        pltpu.VMEM((feat, 2 * width), BF16),
+        pltpu.VMEM((feat, 2 * width), BF16),
+        pltpu.VMEM((1, feat), F32),
+        pltpu.VMEM((steps, feat), BF16),
+        dma((6,)),
         pltpu.VMEM((steps + 3 * SUB, LANE), F32),
         pltpu.VMEM((steps, feat), BF16),
         pltpu.VMEM((steps, feat), BF16),
@@ -418,24 +495,27 @@
         pltpu.VMEM((2, tiles, LANE), F32),
         pltpu.VMEM((4, tiles, LANE), F32),
         pltpu.VMEM((2, feat, steps), F32),
-        pltpu.VMEM((members, feat, steps), F32),
-        pltpu.VMEM((feat, members * steps), BF16),
+        pltpu.VMEM((4, feat, steps), F32),
+        pltpu.VMEM((feat, 4 * steps), BF16),
         pltpu.VMEM((2, 2 * tiles, steps, LANE), F32),
-        pltpu.VMEM((chunks, members, steps, LANE), F32),
+        pltpu.VMEM((2 * chunks, 4, steps, LANE), F32),
         pltpu.VMEM((steps, 2 * width), BF16),
         pltpu.VMEM((steps, 2 * width), BF16),
         pltpu.VMEM((chunks, feat, LANE), F32),
+        pltpu.VMEM((chunks, feat, LANE), F32),
+        pltpu.VMEM((chunks, feat, LANE), F32),
         pltpu.VMEM((chunks, planes, plane_rows, LANE), F32),
         pltpu.VMEM((chunks, planes, plane_rows, LANE), F32),
-        pltpu.VMEM((plane_rows, block), F32),
-        pltpu.VMEM((members, own_rows, block), F32),
-        pltpu.VMEM((members, own_rows, block), F32),
+        pltpu.VMEM((chunks, members, own_rows, LANE), F32),
+        pltpu.VMEM((chunks, members, own_rows, LANE), F32),
         dma((times,)), dma((times,)),
-        dma((members,)), dma((members,)),
+        dma((3,)), dma((3,)),
+        dma((2 * chunks, 3)), dma((2 * chunks, 3)),
+        dma((chunks,)), dma((chunks,)),
+        dma((chunks, planes)), dma((chunks, planes)),
         dma((chunks, members)), dma((chunks, members)),
-        dma((chunks, planes)), dma((chunks, planes)),
-        dma((members,)), dma((members,)),
     ]
+    hbm = pl.BlockSpec(memory_space=pl.ANY)
     out = pl.pallas_call(
         functools.partial(kernel, groups, times),
         out_shape=(
@@ -444,7 +524,7 @@
             jax.ShapeDtypeStruct((own_rows, 2 * width), F32),
             jax.ShapeDtypeStruct((own_rows, 2 * width), F32),
         ),
-        in_specs=[vmem] * 7,
+        in_specs=[hbm, hbm, vmem, hbm, hbm, hbm, hbm],
         out_specs=(vmem,) * 4,
         scratch_shapes=scratch,
         compiler_params=pltpu.CompilerParams(

time: 75.8 us -> 67.5 us (0.89)
  Pallas kernels: 65.1 us -> 56.8 us
    pallas_call x1, Pallas kernels: 65.1 us -> 56.8 us  [body(): pl.pallas_call(functools.partial(kernel, groups, times), out_shape=(jax.S...]
where the time goes in v2:
time: 67.5 us; the launch traced here: 67.2 us
  Pallas kernels  56.8 us (84%)
  local copies, waits for them, and re-layouts  8.94 us (13%)
  other arithmetic  0.76 us (1%)
    pallas_call x1, Pallas kernels, body(): pl.pallas_call(functools.partial(kernel, groups, times), out_shape=(jax.S...  56.8 us
    unnamed x16, local copies, waits for them, and re-layouts  8.94 us

profile of v2, /device:TPU:0, one launch (start us, length us, event | category | flops | bytes accessed | tf_op | source)
XLA Modules:
  0.0 67.2 jit_solution(7224239634744753007)
XLA Ops:
  0.6 0.7 %cosine_multiply_fusion = (f32[1024]{0:T(1024)S(1)}, f32[1024]{0:T(1024)S(1)}, f32[1024]{0:T(1024)S(1)}) fusion(f32[1024]{0:T(1024)} %param.11, f32[1024]{0:T(1024)} %param.10), kind=kLoop, calls=%fused_computation.3 | loop fusion | flops 5120 | bytes 20480 | tf_op jit(solution)/shard_map/mul | solution.py:468
  1.4 0.0 copy-start
  1.4 1.6 %copy-done = bf16[512,2048]{1,0:T(8,128)(2,1)S(1)} copy-done((bf16[512,2048]{1,0:T(8,128)(2,1)S(1)}, bf16[512,2048]{1,0:T(8,128)(2,1)}, u32[]{:S(2)}) %copy-start) | copy-done | bytes 2097176
  3.0 0.0 copy-start.1
  3.0 1.6 %copy-done.1 = bf16[512,2048]{1,0:T(8,128)(2,1)S(1)} copy-done((bf16[512,2048]{1,0:T(8,128)(2,1)S(1)}, bf16[512,2048]{1,0:T(8,128)(2,1)}, u32[]{:S(2)}) %copy-start.1) | copy-done | bytes 2097176
  4.6 0.0 copy-start.2
  4.6 0.9 %copy-done.2 = bf16[1,128,512]{2,1,0:T(8,128)(2,1)S(1)} copy-done((bf16[1,128,512]{2,1,0:T(8,128)(2,1)S(1)}, bf16[1,128,512]{2,1,0:T(8,128)(2,1)}, u32[]{:S(2)}) %copy-start.2) | copy-done | bytes 131096
  5.5 0.0 copy-start.3
  5.5 0.9 %copy-done.3 = bf16[1,128,512]{2,1,0:T(8,128)(2,1)S(1)} copy-done((bf16[1,128,512]{2,1,0:T(8,128)(2,1)S(1)}, bf16[1,128,512]{2,1,0:T(8,128)(2,1)}, u32[]{:S(2)}) %copy-start.3) | copy-done | bytes 131096
  6.4 0.0 copy-start.4
  6.4 0.7 %copy-done.4 = f32[512]{0:T(512)S(1)} copy-done((f32[512]{0:T(512)S(1)}, f32[512]{0:T(512)}, u32[]{:S(2)}) %copy-start.4) | copy-done | bytes 2072
  7.1 0.0 copy-start.5
  7.1 0.7 copy-done.5
  7.7 56.8 %shard_map.111 = (bf16[128,512]{1,0:T(8,128)(2,1)S(1)}, bf16[128,512]{1,0:T(8,128)(2,1)S(1)}, f32[16,2048]{1,0:T(8,128)S(1)}, f32[16,2048]{1,0:T(8,128)S(1)}) custom-call(bf16[128,512]{1,0:T(8,128)(2,1)S(1)} %bitcast.10, f32[1,128]{1,0:T(1,128)S(1)} %copy-done.5, f32[3,1024]{1,0:T(4,128)S(1)} %pad_maximum_fusion.par_ref, bf16[512,2048]{1,0:T(8,128)(2,1)S(1)} %copy-done, ...), custom_call_target="tpu_custom_call" | custom-call | flops 1879048192 | bytes 4194304 | tf_op jit(solution)/shard_map/pallas_call | solution.py:519
  64.5 0.7 copy.16
  65.2 0.7 copy.17
  65.9 0.7 copy.18
  66.5 0.7 copy.19
  (1 shorter events, 0.0 us)
Async XLA Ops:
  1.4 1.6 %copy-start = (bf16[512,2048]{1,0:T(8,128)(2,1)S(1)}, bf16[512,2048]{1,0:T(8,128)(2,1)}, u32[]{:S(2)}) copy-start(bf16[512,2048]{1,0:T(8,128)(2,1)} %win_hbm.1) | copy-start | bytes 6291460
  3.0 1.6 %copy-start.1 = (bf16[512,2048]{1,0:T(8,128)(2,1)S(1)}, bf16[512,2048]{1,0:T(8,128)(2,1)}, u32[]{:S(2)}) copy-start(bf16[512,2048]{1,0:T(8,128)(2,1)} %wout_hbm.1) | copy-start | bytes 6291460
  4.6 0.9 %copy-start.2 = (bf16[1,128,512]{2,1,0:T(8,128)(2,1)S(1)}, bf16[1,128,512]{2,1,0:T(8,128)(2,1)}, u32[]{:S(2)}) copy-start(bf16[1,128,512]{2,1,0:T(8,128)(2,1)} %param.8) | copy-start | bytes 393220
  5.5 0.9 %copy-start.3 = (bf16[1,128,512]{2,1,0:T(8,128)(2,1)S(1)}, bf16[1,128,512]{2,1,0:T(8,128)(2,1)}, u32[]{:S(2)}) copy-start(bf16[1,128,512]{2,1,0:T(8,128)(2,1)} %param.15) | copy-start | bytes 393220
  6.4 0.7 %copy-start.4 = (f32[512]{0:T(512)S(1)}, f32[512]{0:T(512)}, u32[]{:S(2)}) copy-start(f32[512]{0:T(512)} %param.14) | copy-start | bytes 6148
  7.1 0.7 copy-start.5

commit v3 on v2

--- a/solution.py
+++ b/solution.py
@@ -135,7 +135,6 @@
     gamma = par_ref[2:3, :]
     x[:, :width] = gamma * jnp.dot(sigb[...], win_ref[:, :width], preferred_element_type=F32)
     x[:, width:] = gamma * jnp.dot(sigb[...], win_ref[:, width:], preferred_element_type=F32)
-    y[...] = jnp.dot(cotb[...], wout_ref[...], preferred_element_type=F32)
 
     lre = jnp.broadcast_to(par_ref[0:1, :], (SUB, width))
     lim = jnp.broadcast_to(par_ref[1:2, :], (SUB, width))
@@ -162,11 +161,6 @@
         sre, sim = forward_step(j, sre, sim)
     ends[0] = sre
     ends[1] = sim
-    bre, bim = zero, zero
-    for j in reversed(range(inner)):
-        _, _, bre, bim = backward_step(j, bre, bim)
-    ends[2] = bre
-    ends[3] = bim
     prod = dampb[0:SUB, :]
     for j in range(1, inner):
         prod = prod * dampb[rows_of(j), :]
@@ -201,6 +195,41 @@
         ere = here[:, 0:1] * mre + ends[0, one]
         eim = here[:, 0:1] * mim + ends[1, one]
         total = total * here
+    cmsg[0, 2] = jnp.broadcast_to(total, (tiles, LANE))
+    cmsg[1, 2] = jnp.broadcast_to(total, (tiles, LANE))
+    for i in range(tiles):
+        lanes = slice(i * LANE, (i + 1) * LANE)
+        one = slice(i, i + 1)
+        cmsg[0, 0, one] = ere[:, lanes]
+        cmsg[0, 1, one] = eim[:, lanes]
+
+    def carry_copy(q):
+        later = jnp.where(q > t, 0, 1)
+        return pltpu.make_async_remote_copy(
+            src_ref=cmsg.at[later], dst_ref=crecv.at[t],
+            send_sem=csend_sem.at[q], recv_sem=crecv_sem.at[t],
+            device_id=(g, q), device_id_type=MESH,
+        )
+
+    def carry_arrival(q):
+        return pltpu.make_async_remote_copy(
+            src_ref=cmsg.at[0], dst_ref=crecv.at[q],
+            send_sem=csend_sem.at[q], recv_sem=crecv_sem.at[q],
+            device_id=(g, q), device_id_type=MESH,
+        )
+
+    def start_carry(q, carry):
+        carry_copy(q).start()
+        return carry
+
+    lax.fori_loop(t + 1, times, start_carry, 0)
+
+    y[...] = jnp.dot(cotb[...], wout_ref[...], preferred_element_type=F32)
+    bre, bim = zero, zero
+    for j in reversed(range(inner)):
+        _, _, bre, bim = backward_step(j, bre, bim)
+    ends[2] = bre
+    ends[3] = bim
     ore = oim = jnp.zeros((1, width), F32)
     tail = jnp.ones((1, LANE), F32)
     for o in reversed(range(SUB)):
@@ -218,35 +247,12 @@
     for i in range(tiles):
         lanes = slice(i * LANE, (i + 1) * LANE)
         one = slice(i, i + 1)
-        cmsg[0, 0, one] = ere[:, lanes]
-        cmsg[0, 1, one] = eim[:, lanes]
         cmsg[1, 0, one] = ore[:, lanes]
         cmsg[1, 1, one] = oim[:, lanes]
         ldev[0, one] = dre[:, lanes]
         ldev[1, one] = dim[:, lanes]
-    cmsg[0, 2] = jnp.broadcast_to(total, (tiles, LANE))
-    cmsg[1, 2] = jnp.broadcast_to(total, (tiles, LANE))
-
-    def carry_copy(q):
-        later = jnp.where(q > t, 0, 1)
-        return pltpu.make_async_remote_copy(
-            src_ref=cmsg.at[later], dst_ref=crecv.at[t],
-            send_sem=csend_sem.at[q], recv_sem=crecv_sem.at[t],
-            device_id=(g, q), device_id_type=MESH,
-        )
-
-    def carry_arrival(q):
-        return pltpu.make_async_remote_copy(
-            src_ref=cmsg.at[0], dst_ref=crecv.at[q],
-            send_sem=csend_sem.at[q], recv_sem=crecv_sem.at[q],
-            device_id=(g, q), device_id_type=MESH,
-        )
-
-    def start_carry(d, carry):
-        carry_copy((t + d) % times).start()
-        return carry
-
-    lax.fori_loop(1, times, start_carry, 0)
+
+    lax.fori_loop(0, t, start_carry, 0)
 
     def ahead(q, carry):
         carry_arrival(q).wait_recv()
@@ -264,7 +270,6 @@
 
     none = jnp.zeros((tiles, LANE), F32)
     cfull[0], cfull[1] = lax.fori_loop(0, t, ahead, (none, none))
-    cfull[2], cfull[3] = lax.fori_loop(0, times - 1 - t, behind, (none, none))
 
     def wide(i):
         return jnp.concatenate([cfull[i, k : k + 1, :] for k in range(tiles)], axis=1)
@@ -296,20 +301,23 @@
             device_id=(device, z * 2 + kind), device_id_type=MESH,
         )
 
+    early = min(4, units)
+
     def start_drive(kind):
         @pl.when(c == kind)
         def _():
-            for u in range(units):
+            for u in range(early):
                 drive_copy(u, 0).start()
 
         @pl.when(c != kind)
         def _():
-            for u in range(units):
+            for u in range(early):
                 drive_copy(u, 2).start()
                 drive_copy(u, 1).start()
 
     start_drive(1)
 
+    cfull[2], cfull[3] = lax.fori_loop(0, times - 1 - t, behind, (none, none))
     kre, kim = wide(2), wide(3)
     mre = tre * kre + tim * kim
     mim = tre * kim - tim * kre
@@ -328,19 +336,6 @@
     for u in range(units):
         dgat[u, own_slot] = dsend[c, unit_column(u, g, c)]
 
-    for i in range(2 * tiles):
-        lanes = slice(i * LANE, (i + 1) * LANE)
-        packed[:, lanes] = dsend[1, i].astype(BF16)
-        drive[:, lanes] = dsend[0, i].astype(BF16)
-
-    turned = (((1,), (1,)), ((), ()))
-    out = lax.dot_general(packed[...], wout_ref[...], turned, preferred_element_type=F32)
-    out = (out + skip_ref[...] * sigb[...].astype(F32)).astype(BF16)
-    mixed_ref[...] = jnp.dot(restore, out, preferred_element_type=F32).astype(BF16)
-    out = lax.dot_general(drive[...], win_ref[...], turned, preferred_element_type=F32)
-    out = (out + skip_ref[...] * cotb[...].astype(F32)).astype(BF16)
-    gsig_ref[...] = jnp.dot(restore, out, preferred_element_type=F32).astype(BF16)
-
     for d in range(3):
         factor_copy(d).wait_recv()
     for m in range(4):
@@ -421,9 +416,25 @@
             gin_ref[:, lanes] = ogat[k, gg * 2]
             gout_ref[:, lanes] = ogat[k, gg * 2 + 1]
 
+    turned = (((1,), (1,)), ((), ()))
+
+    def mix(kind, bits, weight, skipped, result):
+        for i in range(2 * tiles):
+            bits[:, i * LANE : (i + 1) * LANE] = dsend[kind, i].astype(BF16)
+        out = lax.dot_general(bits[...], weight[...], turned, preferred_element_type=F32)
+        out = (out + skip_ref[...] * skipped[...].astype(F32)).astype(BF16)
+        result[...] = jnp.dot(restore, out, preferred_element_type=F32).astype(BF16)
+
     for s in range(chunks + 4):
         if s < chunks:
             multiply(s)
+            for u in range(early + 2 * s, min(early + 2 * s + 2, units)):
+                for d in (0, 2, 1):
+                    drive_copy(u, d).start()
+        if s == 0:
+            mix(1, packed, wout_ref, sigb, mixed_ref)
+        if s == min(1, chunks - 1):
+            mix(0, drive, win_ref, cotb, gsig_ref)
         if 0 <= s - 1 < chunks:
             add_partner(s - 1)
         if 0 <= s - 3 < chunks:
@@ -515,7 +526,7 @@
         dma((chunks, planes)), dma((chunks, planes)),
         dma((chunks, members)), dma((chunks, members)),
     ]
-    hbm = pl.BlockSpec(memory_space=pl.ANY)
+    hbm = pl.BlockSpec(memory_space=pltpu.HBM)
     out = pl.pallas_call(
         functools.partial(kernel, groups, times),
         out_shape=(
@@ -528,7 +539,7 @@
         out_specs=(vmem,) * 4,
         scratch_shapes=scratch,
         compiler_params=pltpu.CompilerParams(
-            collective_id=0, has_side_effects=True, vmem_limit_bytes=48 * 1024 * 1024
+            collective_id=0, has_side_effects=True, vmem_limit_bytes=60 * 1024 * 1024
         ),
         cost_estimate=pl.CostEstimate(
             flops=14 * steps * feat * 2 * width, bytes_accessed=8 * feat * width, transcendentals=0

time: 67.5 us -> 62.7 us (0.929)
  Pallas kernels: 56.8 us -> 54.1 us
  local copies, waits for them, and re-layouts: 8.94 us -> 6.27 us
    unnamed x16 -> x4, local copies, waits for them, and re-layouts: 8.94 us -> 6.27 us
    pallas_call x1, Pallas kernels: 56.8 us -> 54.1 us  [body(): pl.pallas_call(functools.partial(kernel, groups, times), out_shape=(jax.S...]
where the time goes in v3:
time: 62.7 us; the launch traced here: 62.4 us
  Pallas kernels  54.1 us (86%)
  local copies, waits for them, and re-layouts  6.27 us (10%)
  other arithmetic  1.37 us (2%)
  between operations  0.64 us (1%)
    pallas_call x1, Pallas kernels, body(): pl.pallas_call(functools.partial(kernel, groups, times), out_shape=(jax.S...  54.1 us
    unnamed x4, local copies, waits for them, and re-layouts  6.27 us

profile of v3, /device:TPU:0, one launch (start us, length us, event | category | flops | bytes accessed | tf_op | source)
XLA Modules:
  0.0 62.4 jit_solution(7561397946764692551)
XLA Ops:
  0.6 0.7 %cosine_multiply_fusion = (f32[1024]{0:T(1024)S(1)}, f32[1024]{0:T(1024)S(1)}, f32[1024]{0:T(1024)S(1)}) fusion(f32[1024]{0:T(1024)} %param.11, f32[1024]{0:T(1024)} %param.10), kind=kLoop, calls=%fused_computation.3 | loop fusion | flops 5120 | bytes 20480 | tf_op jit(solution)/shard_map/mul | solution.py:479
  1.4 0.6 %pad_maximum_fusion.par_ref = f32[3,1024]{1,0:T(4,128)} fusion(f32[1,1024]{1,0:T(1,128)S(1)} %bitcast.12, f32[1,1024]{1,0:T(1,128)S(1)} %bitcast.11, f32[1,1024]{1,0:T(1,128)S(1)} %bitcast.10), kind=kLoop, calls=%fused_computation | loop fusion | flops 6144 | bytes 24576 | tf_op jit(solution)/shard_map/stack | solution.py:479
  2.0 54.1 %shard_map.111 = (bf16[128,512]{1,0:T(8,128)(2,1)}, bf16[128,512]{1,0:T(8,128)(2,1)}, f32[16,2048]{1,0:T(8,128)}, f32[16,2048]{1,0:T(8,128)}) custom-call(bf16[128,512]{1,0:T(8,128)(2,1)} %bitcast.13, f32[1,128]{1,0:T(1,128)} %damp_hbm.1, f32[3,1024]{1,0:T(4,128)} %pad_maximum_fusion.par_ref, bf16[512,2048]{1,0:T(8,128)(2,1)} %win_hbm.1, ...), custom_call_target="tpu_custom_call" | custom-call | flops 1879048192 | bytes 4194304 | tf_op jit(solution)/shard_map/pallas_call | solution.py:530
  56.2 1.6 %copy.16 = bf16[1,128,512]{2,1,0:T(8,128)(2,1)} copy(bf16[1,128,512]{2,1,0:T(8,128)(2,1)} %bitcast.9) | data formatting | bytes 262144
  57.7 1.6 %copy.17 = bf16[1,128,512]{2,1,0:T(8,128)(2,1)} copy(bf16[1,128,512]{2,1,0:T(8,128)(2,1)} %bitcast.8) | data formatting | bytes 262144
  59.3 1.6 %copy.18 = f32[16,2048]{1,0:T(8,128)} copy(f32[16,2048]{1,0:T(8,128)} %get-tuple-element.21) | data formatting | bytes 262144
  60.9 1.6 %copy.19 = f32[16,2048]{1,0:T(8,128)} copy(f32[16,2048]{1,0:T(8,128)} %get-tuple-element.22) | data formatting | bytes 262144

commit v4 on v3

--- a/solution.py
+++ b/solution.py
@@ -27,16 +27,16 @@
 
 def kernel(
     groups, times,
-    sig_hbm, damp_hbm, par_ref, win_hbm, wout_hbm, skip_hbm, cot_hbm,
+    sig_hbm, damp_hbm, lre_ref, lim_ref, gamma_ref, win_hbm, wout_hbm, skip_hbm, cot_hbm,
     mixed_ref, gsig_ref, gin_ref, gout_ref,
     sig_ref, damp_ref, win_ref, wout_ref, skip_ref, cot_ref, load_sem,
     dampb, sigb, cotb, x, y, ends, enters, cmsg, crecv, ldev, cfull,
-    fsend, fgat, factor, dsend, dgat, packed, drive, pbuf, rsend, rgat, zsend, zgat, osend, ogat,
+    fsend, fgat, factor, dsend, dgat, packed, drive, pbuf, rsend, rgat, zsend, zgat, hsend, hgat, osend, ogat,
     csend_sem, crecv_sem, fsend_sem, frecv_sem, dsend_sem, drecv_sem,
     rsend_sem, rrecv_sem, zsend_sem, zrecv_sem, osend_sem, orecv_sem,
 ):
     steps, feat = sig_hbm.shape
-    width = par_ref.shape[1]
+    width = lre_ref.shape[1]
     inner = steps // SUB
     planes = times // 2
     members = groups * 2
@@ -46,6 +46,7 @@
     own_rows = feat // (groups * times)
     pair_rows = 2 * own_rows
     units = 2 * chunks
+    half = planes // 2
 
     g = lax.axis_index("grp")
     t = lax.axis_index("tm")
@@ -132,12 +133,12 @@
 
     for load in loads[3:]:
         load.wait()
-    gamma = par_ref[2:3, :]
+    gamma = gamma_ref[...]
     x[:, :width] = gamma * jnp.dot(sigb[...], win_ref[:, :width], preferred_element_type=F32)
     x[:, width:] = gamma * jnp.dot(sigb[...], win_ref[:, width:], preferred_element_type=F32)
 
-    lre = jnp.broadcast_to(par_ref[0:1, :], (SUB, width))
-    lim = jnp.broadcast_to(par_ref[1:2, :], (SUB, width))
+    lre = jnp.broadcast_to(lre_ref[...], (SUB, width))
+    lim = jnp.broadcast_to(lim_ref[...], (SUB, width))
 
     def rows_of(j):
         return slice(j * SUB, (j + 1) * SUB)
@@ -166,7 +167,7 @@
         prod = prod * dampb[rows_of(j), :]
     dampb[steps : steps + SUB, :] = prod
 
-    one_re, one_im = square_times(par_ref[0:1, :], par_ref[1:2, :], inner)
+    one_re, one_im = square_times(lre_ref[...], lim_ref[...], inner)
     place = lax.broadcasted_iota(jnp.int32, (SUB, width), 0)
 
     def edge_power(index):
@@ -348,12 +349,22 @@
             device_id=(flipped(g, c), t), device_id_type=MESH,
         )
 
+    parity = z % 2
+    rank = z // 2
+
+    def next_copy(k):
+        return pltpu.make_async_remote_copy(
+            src_ref=zsend.at[k, 1 - parity], dst_ref=zgat.at[k],
+            send_sem=zsend_sem.at[k, 0], recv_sem=zrecv_sem.at[k, 0],
+            device_id=(g, (rank * 2 + 1 - parity) * 2 + c), device_id_type=MESH,
+        )
+
     def plane_copy(k, d):
-        other = (z + d) % planes
-        return pltpu.make_async_remote_copy(
-            src_ref=zsend.at[k, other], dst_ref=zgat.at[k, z],
+        other = (rank + d) % half
+        return pltpu.make_async_remote_copy(
+            src_ref=hsend.at[k, other], dst_ref=hgat.at[k, rank],
             send_sem=zsend_sem.at[k, d], recv_sem=zrecv_sem.at[k, d],
-            device_id=(g, other * 2 + c), device_id_type=MESH,
+            device_id=(g, (other * 2 + parity) * 2 + c), device_id_type=MESH,
         )
 
     def owner_copy(k, d):
@@ -381,20 +392,26 @@
             for zz in range(planes):
                 first = gg * times * own_rows + zz * pair_rows
                 rows = slice(first, first + pair_rows)
-                zsend[k, zz, gg * pair_rows : (gg + 1) * pair_rows] = pbuf[k, rows] + rgat[k, rows]
+                place = slice(gg * pair_rows, (gg + 1) * pair_rows)
+                zsend[k, zz % 2, zz // 2, place] = pbuf[k, rows] + rgat[k, rows]
+        next_copy(k).start()
+
+    def add_next(k):
+        next_copy(k).wait_recv()
+        hsend[k] = zsend[k, parity] + zgat[k]
 
         def start_plane(d, carry):
             plane_copy(k, d).start()
             return carry
 
-        lax.fori_loop(1, planes, start_plane, 0)
+        lax.fori_loop(1, half, start_plane, 0)
 
     def add_planes(k):
         def add_plane(d, acc):
             plane_copy(k, d).wait_recv()
-            return acc + zgat[k, (z + planes - d) % planes]
-
-        pbuf[k, : members * own_rows] = lax.fori_loop(1, planes, add_plane, zsend[k, z])
+            return acc + hgat[k, (rank + half - d) % half]
+
+        pbuf[k, : members * own_rows] = lax.fori_loop(1, half, add_plane, hsend[k, rank])
         for m in range(members):
             osend[k, m] = pbuf[k, m * own_rows : (m + 1) * own_rows]
 
@@ -431,16 +448,19 @@
             for u in range(early + 2 * s, min(early + 2 * s + 2, units)):
                 for d in (0, 2, 1):
                     drive_copy(u, d).start()
+        if 0 <= s - 1 < chunks:
+            add_partner(s - 1)
+        if 0 <= s - 2 < chunks:
+            add_next(s - 2)
         if s == 0:
             mix(1, packed, wout_ref, sigb, mixed_ref)
-        if s == min(1, chunks - 1):
+        if s == 1:
             mix(0, drive, win_ref, cotb, gsig_ref)
-        if 0 <= s - 1 < chunks:
-            add_partner(s - 1)
-        if 0 <= s - 3 < chunks:
-            add_planes(s - 3)
         if 0 <= s - 4 < chunks:
-            finish(s - 4)
+            add_planes(s - 4)
+        if 0 <= s - 5 < chunks:
+            finish(s - 5)
+    finish(chunks - 1)
 
     for d in range(3):
         factor_copy(d).wait_send()
@@ -461,13 +481,27 @@
             plane_copy(k, d).wait_send()
         return carry
 
-    lax.fori_loop(1, planes, drain_planes, 0)
+    lax.fori_loop(1, half, drain_planes, 0)
+    for k in range(chunks):
+        next_copy(k).wait_send()
 
     def drain_times(d, carry):
         carry_copy((t + d) % times).wait_send()
         return carry
 
     lax.fori_loop(1, times, drain_times, 0)
+
+
+def write_out(*refs):
+    count = len(refs) // 2
+    sources, results, sem = refs[:count], refs[count : 2 * count], refs[-1]
+    copies = [
+        pltpu.make_async_copy(a, b, sem.at[i]) for i, (a, b) in enumerate(zip(sources, results))
+    ]
+    for copy in copies:
+        copy.start()
+    for copy in copies:
+        copy.wait()
 
 
 def body(groups, times, signal, damping, nu_log, theta, in_weight, out_weight, skip_gain, cotangent):
@@ -476,7 +510,8 @@
     rate = jnp.exp(nu_log)
     magnitude = jnp.exp(-rate)
     scaling = jnp.sqrt(-jnp.expm1(-2.0 * rate))
-    par = jnp.stack([magnitude * jnp.cos(theta), magnitude * jnp.sin(theta), scaling], 0)
+    lam_re = magnitude * jnp.cos(theta)
+    lam_im = magnitude * jnp.sin(theta)
     members = groups * 2
     planes = times // 2
     block = 2 * width // groups
@@ -515,15 +550,17 @@
         pltpu.VMEM((chunks, feat, LANE), F32),
         pltpu.VMEM((chunks, feat, LANE), F32),
         pltpu.VMEM((chunks, feat, LANE), F32),
-        pltpu.VMEM((chunks, planes, plane_rows, LANE), F32),
-        pltpu.VMEM((chunks, planes, plane_rows, LANE), F32),
+        pltpu.VMEM((chunks, 2, planes // 2, plane_rows, LANE), F32),
+        pltpu.VMEM((chunks, planes // 2, plane_rows, LANE), F32),
+        pltpu.VMEM((chunks, planes // 2, plane_rows, LANE), F32),
+        pltpu.VMEM((chunks, planes // 2, plane_rows, LANE), F32),
         pltpu.VMEM((chunks, members, own_rows, LANE), F32),
         pltpu.VMEM((chunks, members, own_rows, LANE), F32),
         dma((times,)), dma((times,)),
         dma((3,)), dma((3,)),
         dma((2 * chunks, 3)), dma((2 * chunks, 3)),
         dma((chunks,)), dma((chunks,)),
-        dma((chunks, planes)), dma((chunks, planes)),
+        dma((chunks, planes // 2)), dma((chunks, planes // 2)),
         dma((chunks, members)), dma((chunks, members)),
     ]
     hbm = pl.BlockSpec(memory_space=pltpu.HBM)
@@ -535,7 +572,7 @@
             jax.ShapeDtypeStruct((own_rows, 2 * width), F32),
             jax.ShapeDtypeStruct((own_rows, 2 * width), F32),
         ),
-        in_specs=[hbm, hbm, vmem, hbm, hbm, hbm, hbm],
+        in_specs=[hbm, hbm, vmem, vmem, vmem, hbm, hbm, hbm, hbm],
         out_specs=(vmem,) * 4,
         scratch_shapes=scratch,
         compiler_params=pltpu.CompilerParams(
@@ -544,7 +581,16 @@
         cost_estimate=pl.CostEstimate(
             flops=14 * steps * feat * 2 * width, bytes_accessed=8 * feat * width, transcendentals=0
         ),
-    )(signal[0], damping, par, in_weight, out_weight, skip_gain[None], cotangent[0])
+    )(signal[0], damping, lam_re[None], lam_im[None], scaling[None], in_weight, out_weight, skip_gain[None], cotangent[0])
+    anywhere = pl.BlockSpec(memory_space=pl.ANY)
+    out = pl.pallas_call(
+        write_out,
+        out_shape=tuple(jax.ShapeDtypeStruct(a.shape, a.dtype) for a in out),
+        in_specs=[anywhere] * 4,
+        out_specs=(anywhere,) * 4,
+        scratch_shapes=[dma((4,))],
+        compiler_params=pltpu.CompilerParams(vmem_limit_bytes=60 * 1024 * 1024),
+    )(*out)
     return (out[0][None], out[1][None], out[2], out[3])
 
 

time: 62.7 us -> 73.2 us (1.17)
  Pallas kernels: 54.1 us -> 70.9 us
  local copies, waits for them, and re-layouts: 6.27 us -> 0 us
    pallas_call x0 -> x1, Pallas kernels: none -> 17 us  [body(): pl.pallas_call(write_out, out_shape=tuple((jax.ShapeDtypeStruct(a.shape,...]
    unnamed x4 -> x0, local copies, waits for them, and re-layouts: 6.27 us -> none
where the time goes in v4:
time: 73.2 us; the launch traced here: 72.9 us
  Pallas kernels  70.9 us (97%)
  other arithmetic  1.35 us (2%)
    pallas_call x1, Pallas kernels, body(): pl.pallas_call(functools.partial(kernel, groups, times), out_shape=(jax.S...  53.9 us
    pallas_call x1, Pallas kernels, body(): pl.pallas_call(write_out, out_shape=tuple((jax.ShapeDtypeStruct(a.shape,...  17 us

profile of v4, /device:TPU:0, one launch (start us, length us, event | category | flops | bytes accessed | tf_op | source)
XLA Modules:
  0.0 72.9 jit_solution(14459180806672974351)
XLA Ops:
  0.6 1.3 %sine_multiply_fusion = (f32[1024]{0:T(1024)}, f32[1024]{0:T(1024)}, f32[1024]{0:T(1024)}) fusion(f32[1024]{0:T(1024)} %param.11, f32[1024]{0:T(1024)} %param.10), kind=kLoop, calls=%fused_computation.1 | loop fusion | flops 5120 | bytes 20480 | tf_op jit(solution)/shard_map/mul | solution.py:514
  2.0 53.9 %shard_map.111 = (bf16[128,512]{1,0:T(8,128)(2,1)}, bf16[128,512]{1,0:T(8,128)(2,1)}, f32[16,2048]{1,0:T(8,128)}, f32[16,2048]{1,0:T(8,128)}) custom-call(bf16[128,512]{1,0:T(8,128)(2,1)} %bitcast.11, f32[1,128]{1,0:T(1,128)} %damp_hbm.1, f32[1,1024]{1,0:T(1,128)} %bitcast.9, f32[1,1024]{1,0:T(1,128)} %bitcast.8, f32[1,1024]{1,0:T(1,128)} %bitcast.10, ...), custom_call_target="tpu_custom_call" | custom-call | flops 1879048192 | bytes 4194304 | tf_op jit(solution)/shard_map/pallas_call | solution.py:567
  55.9 17.0 %shard_map.112 = (bf16[128,512]{1,0:T(8,128)(2,1)}, bf16[128,512]{1,0:T(8,128)(2,1)}, f32[16,2048]{1,0:T(8,128)}, f32[16,2048]{1,0:T(8,128)}) custom-call(bf16[128,512]{1,0:T(8,128)(2,1)} %get-tuple-element.12.refs_0_, bf16[128,512]{1,0:T(8,128)(2,1)} %get-tuple-element.13.refs_1_, f32[16,2048]{1,0:T(8,128)} %get-tuple-element.14.refs_2_, ...), custom_call_target="tpu_custom_call" | custom-call | tf_op jit(solution)/shard_map/pallas_call | solution.py:586

commit v5 on v4

--- a/solution.py
+++ b/solution.py
@@ -494,14 +494,8 @@
 
 def write_out(*refs):
     count = len(refs) // 2
-    sources, results, sem = refs[:count], refs[count : 2 * count], refs[-1]
-    copies = [
-        pltpu.make_async_copy(a, b, sem.at[i]) for i, (a, b) in enumerate(zip(sources, results))
-    ]
-    for copy in copies:
-        copy.start()
-    for copy in copies:
-        copy.wait()
+    for source, result in zip(refs[:count], refs[count:]):
+        result[...] = source[...]
 
 
 def body(groups, times, signal, damping, nu_log, theta, in_weight, out_weight, skip_gain, cotangent):
@@ -582,13 +576,11 @@
             flops=14 * steps * feat * 2 * width, bytes_accessed=8 * feat * width, transcendentals=0
         ),
     )(signal[0], damping, lam_re[None], lam_im[None], scaling[None], in_weight, out_weight, skip_gain[None], cotangent[0])
-    anywhere = pl.BlockSpec(memory_space=pl.ANY)
     out = pl.pallas_call(
         write_out,
         out_shape=tuple(jax.ShapeDtypeStruct(a.shape, a.dtype) for a in out),
-        in_specs=[anywhere] * 4,
-        out_specs=(anywhere,) * 4,
-        scratch_shapes=[dma((4,))],
+        in_specs=[vmem] * 4,
+        out_specs=(vmem,) * 4,
         compiler_params=pltpu.CompilerParams(vmem_limit_bytes=60 * 1024 * 1024),
     )(*out)
     return (out[0][None], out[1][None], out[2], out[3])

time: 73.2 us -> 58.1 us (0.79)
  Pallas kernels: 70.9 us -> 55.8 us
    pallas_call x1, Pallas kernels: 17 us -> 1.89 us  [body(): pl.pallas_call(write_out, out_shape=tuple((jax.ShapeDtypeStruct(a.shape,...]
where the time goes in v5:
time: 58.1 us; the launch traced here: 57.8 us
  Pallas kernels  55.8 us (96%)
  other arithmetic  1.35 us (2%)
  between operations  0.64 us (1%)
    pallas_call x1, Pallas kernels, body(): pl.pallas_call(functools.partial(kernel, groups, times), out_shape=(jax.S...  53.9 us
    pallas_call x1, Pallas kernels, body(): pl.pallas_call(write_out, out_shape=tuple((jax.ShapeDtypeStruct(a.shape,...  1.89 us
    mul x1, other arithmetic, body(): lam_im = magnitude * jnp.sin(theta)  1.35 us

profile of v5, /device:TPU:0, one launch (start us, length us, event | category | flops | bytes accessed | tf_op | source)
XLA Modules:
  0.0 57.8 jit_solution(90243918358753936)
XLA Ops:
  0.6 1.3 %sine_multiply_fusion = (f32[1024]{0:T(1024)}, f32[1024]{0:T(1024)}, f32[1024]{0:T(1024)}) fusion(f32[1024]{0:T(1024)} %param.11, f32[1024]{0:T(1024)} %param.10), kind=kLoop, calls=%fused_computation.1 | loop fusion | flops 5120 | bytes 20480 | tf_op jit(solution)/shard_map/mul | solution.py:508
  2.0 53.9 %shard_map.111 = (bf16[128,512]{1,0:T(8,128)(2,1)}, bf16[128,512]{1,0:T(8,128)(2,1)}, f32[16,2048]{1,0:T(8,128)}, f32[16,2048]{1,0:T(8,128)}) custom-call(bf16[128,512]{1,0:T(8,128)(2,1)} %bitcast.11, f32[1,128]{1,0:T(1,128)} %damp_hbm.1, f32[1,1024]{1,0:T(1,128)} %bitcast.9, f32[1,1024]{1,0:T(1,128)} %bitcast.8, f32[1,1024]{1,0:T(1,128)} %bitcast.10, ...), custom_call_target="tpu_custom_call" | custom-call | flops 1879048192 | bytes 4194304 | tf_op jit(solution)/shard_map/pallas_call | solution.py:561
  55.9 1.9 %shard_map.112 = (bf16[128,512]{1,0:T(8,128)(2,1)}, bf16[128,512]{1,0:T(8,128)(2,1)}, f32[16,2048]{1,0:T(8,128)}, f32[16,2048]{1,0:T(8,128)}) custom-call(bf16[128,512]{1,0:T(8,128)(2,1)} %get-tuple-element.12.refs_0_, bf16[128,512]{1,0:T(8,128)(2,1)} %get-tuple-element.13.refs_1_, f32[16,2048]{1,0:T(8,128)} %get-tuple-element.14.refs_2_, ...), custom_call_target="tpu_custom_call" | custom-call | tf_op jit(solution)/shard_map/pallas_call | solution.py:579
